TPU v7x, 256 devices: a whole 4x4x8 slice. The times are simulated.
256 devices in a mesh: pulse: 8 (over y, z_hi), range: 32 (over z_lo, x, core).
Axes of the slice: x: 4, y: 4, z: 8 (z_hi: 2, z_lo: 4; z = z_hi * 4 + z_lo), core: 2. Of those that a mesh axis runs over, the one named last changes fastest.
Arguments:
- phase_real: float32 [8192, 16384], P('pulse', 'range'), may hold values from -6 to 6
- phase_imag: float32 [8192, 16384], P('pulse', 'range'), may hold values from -6 to 6
- interp_tiles: float32 [64, 5, 128, 128], P('pulse'), may hold values from -0.25 to 0.25
- tile_index: int32 [64, 5], P('pulse'), may hold values from -2 to 65, as said below
- tile_count: int32 [64], P('pulse'), may hold values from 3 to 5
Outputs:
- image_real: float32 [8192, 16384], P(('pulse', 'range'))
- image_imag: float32 [8192, 16384], P(('pulse', 'range'))
Inputs may be any that keep to these rules, and one draw needn't show every extreme that they name: `tile_index`: for output block b, slots 0 to 2 name blocks b - 1, b and b + 1 in some order, and slots 3 and 4 name blocks b - 2 and b + 2 in some order; names outside 0 to 63 stand for zero blocks.
All inputs are finite; a program needn't handle non-finite values.
Results may differ from a plain program's by a relative error of at most 0.0001.
Values sent between devices are 32-bit elements; how exact they have to be, the bound alone decides.
No kernel may reach another device: no remote copies, remote signals or barrier semaphores. Data moves between devices by JAX's collectives and lax.ppermute only.
A program may use at most 128 MiB of HBM per device.

v0:
```python
import functools
import math

import jax
import jax.numpy as jnp
import ml_dtypes
import numpy as np
from jax import lax
from jax.experimental import pallas as pl
from jax.experimental.pallas import tpu as pltpu
from jax.sharding import PartitionSpec as P

S = 16384
AZ = 1024
BLOCK = 128
SLOTS = 5
HALO = 2 * BLOCK
LANES = 128
PARTS = (2, 2)
GROUPS = 4
ALL = tuple(range(32))
ONE_CORE = tuple(range(0, 32, 2))
MIDDLE = tuple(r for r in ONE_CORE if r // 8 in (1, 2))
RELAYS = (
    (2, 0, 1, ALL),
    (5, 7, 6, ALL),
    (3, 5, 4, ONE_CORE),
    (4, 2, 3, ONE_CORE),
    (1, 3, 2, MIDDLE),
    (6, 4, 5, MIDDLE),
)
BF16 = jnp.bfloat16
F32 = jnp.float32


def unit_roots(numerators, length):
    angles = 2.0 * math.pi * (numerators % length) / length
    return np.cos(angles), -np.sin(angles)


def halves(table):
    high = table.astype(ml_dtypes.bfloat16)
    low = (table - high.astype(np.float64)).astype(ml_dtypes.bfloat16)
    return high, low


def azimuth_tables():
    idx = np.arange(256)
    real, imag = unit_roots(idx[:, None] * idx[None, :], 256)
    high, low = halves(np.concatenate([real, imag], axis=0) / 32.0)
    turns = []
    for a in range(1, 4):
        turn = np.stack(unit_roots(a * idx, 1024))
        turns.append(np.broadcast_to(turn[:, :, None], (2, 256, LANES)))
    return high, low, np.stack(turns).astype(np.float32)


def range_tables(parts):
    idx = np.arange(128)
    order = []
    first = 0
    for width in parts:
        for source in range(32):
            order += [4 * source + first + c for c in range(width)]
        first += width
    order = np.array(order)
    real, imag = unit_roots(idx[:, None] * order[None, :], 128)
    inner = np.block([[real, -imag], [imag, real]])
    turn = np.stack(unit_roots(idx[:, None] * idx[None, :], S)).astype(np.float32)
    real, imag = unit_roots(idx[:, None] * idx[None, :], 128)
    outer = np.block([[real, -imag], [imag, real]]) / 128.0
    return (*halves(inner), turn, *halves(outer))


def split(value):
    high = value.astype(BF16)
    return high, (value - high.astype(F32)).astype(BF16)


def dot(a, b, dims=(((1,), (0,)), ((), ()))):
    return lax.dot_general(a, b, dims, preferred_element_type=F32)


def azimuth_kernel(re_ref, im_ref, top_ref, bot_ref, wh_ref, wl_ref, dh_ref, dl_ref, tw_ref, out_ref, xh, xl, yh, yl):
    def put(row, real, imag):
        high, low = split(jnp.concatenate([real, imag], axis=1))
        xh[row : row + BLOCK, :] = high
        xl[row : row + BLOCK, :] = low

    for i in range(2):
        rows = slice(i * BLOCK, (i + 1) * BLOCK)
        put(i * BLOCK, top_ref[0, rows], top_ref[1, rows])
        put(HALO + AZ + i * BLOCK, bot_ref[0, rows], bot_ref[1, rows])
    for i in range(AZ // BLOCK):
        rows = slice(i * BLOCK, (i + 1) * BLOCK)
        put(HALO + i * BLOCK, re_ref[rows], im_ref[rows])
    for b in range(AZ // BLOCK):
        rows = slice(b * BLOCK, (b + SLOTS) * BLOCK)
        cells = dot(wh_ref[b], xh[rows]) + dot(wl_ref[b], xh[rows]) + dot(wh_ref[b], xl[rows])
        high, low = split(cells)
        for a in range(4):
            yh[a, b * 32 : (b + 1) * 32] = high[a * 32 : (a + 1) * 32]
            yl[a, b * 32 : (b + 1) * 32] = low[a * 32 : (a + 1) * 32]
    real, imag = [], []
    for a in range(4):
        four = dot(dh_ref[...], yh[a]) + dot(dl_ref[...], yh[a]) + dot(dh_ref[...], yl[a])
        vr = four[:256, :LANES] - four[256:, LANES:]
        vi = four[:256, LANES:] + four[256:, :LANES]
        if a:
            tr, ti = tw_ref[a - 1, 0], tw_ref[a - 1, 1]
            vr, vi = vr * tr - vi * ti, vr * ti + vi * tr
        real.append(vr)
        imag.append(vi)
    er, ei, fr, fi = real[0] + real[2], imag[0] + imag[2], real[0] - real[2], imag[0] - imag[2]
    gr, gi, hr, hi = real[1] + real[3], imag[1] + imag[3], real[1] - real[3], imag[1] - imag[3]
    bins = [(er + gr, ei + gi), (fr + hi, fi - hr), (er - gr, ei - gi), (fr - hi, fi + hr)]
    for quarter in range(4):
        for part in range(2):
            for t in range(8):
                out_ref[quarter * 8 + t, 0, part] = bins[quarter][part][t * 32 : (t + 1) * 32]


def azimuth(first, width, phase_real, phase_imag, top, bot, weights, tables):
    fixed = lambda *shape: pl.BlockSpec(shape, lambda i: (0,) * len(shape))
    return pl.pallas_call(
        azimuth_kernel,
        grid=(width,),
        in_specs=[
            pl.BlockSpec((AZ, LANES), lambda i: (0, first + i)),
            pl.BlockSpec((AZ, LANES), lambda i: (0, first + i)),
            pl.BlockSpec((2, HALO, LANES), lambda i: (0, 0, i)),
            pl.BlockSpec((2, HALO, LANES), lambda i: (0, 0, i)),
            fixed(8, BLOCK, SLOTS * BLOCK),
            fixed(8, BLOCK, SLOTS * BLOCK),
            fixed(512, 256),
            fixed(512, 256),
            fixed(3, 2, 256, LANES),
        ],
        out_specs=pl.BlockSpec((32, 1, 2, 32, LANES), lambda i: (0, i, 0, 0, 0)),
        out_shape=jax.ShapeDtypeStruct((32, width, 2, 32, LANES), F32),
        scratch_shapes=[
            pltpu.VMEM((AZ + 2 * HALO, 2 * LANES), BF16),
            pltpu.VMEM((AZ + 2 * HALO, 2 * LANES), BF16),
            pltpu.VMEM((4, 256, 2 * LANES), BF16),
            pltpu.VMEM((4, 256, 2 * LANES), BF16),
        ],
        compiler_params=pltpu.CompilerParams(vmem_limit_bytes=40 * 1024 * 1024),
        cost_estimate=pl.CostEstimate(
            flops=6 * width * 256 * (AZ * 640 + AZ * 512) * (100 if first else 1), bytes_accessed=width * 2 * 2**20, transcendentals=0
        ),
        name="azimuth",
    )(phase_real, phase_imag, top, bot, *weights, *tables)


def range_kernel(parts, *refs):
    cells = refs[: len(parts)]
    ah_ref, al_ref, tw_ref, bh_ref, bl_ref, re_ref, im_ref = refs[len(parts) :]
    images = [ref.reshape(128 * 8, LANES) for ref in (re_ref, im_ref)]
    inner_table = jnp.concatenate([ah_ref[...], al_ref[...], ah_ref[...]], axis=1)
    outer_table = jnp.concatenate([bh_ref[...], bl_ref[...]], axis=0)
    flat = [ref.reshape(32 * width * 16, LANES) for ref, width in zip(cells, parts)]

    def rows_of(part, k):
        return jnp.concatenate(
            [ref[pl.ds(part * 8 + k, 32 * width, stride=16), :] for ref, width in zip(flat, parts)], axis=0
        )

    tr, ti = tw_ref[0], tw_ref[1]
    for pair in range(4):
        k0, k1 = 2 * pair, 2 * pair + 1
        full = jnp.concatenate(
            [jnp.concatenate([rows_of(part, k) for k in (k0, k1)], axis=1) for part in range(2)], axis=0
        )
        high, low = split(full)
        inner = dot(inner_table, jnp.concatenate([high, high, low], axis=0))
        turned = []
        for i in range(2):
            yr, yi = inner[:128, i * LANES : (i + 1) * LANES], inner[128:, i * LANES : (i + 1) * LANES]
            turned.append(jnp.concatenate([yr * tr - yi * ti, yr * ti + yi * tr], axis=1))
        high, low = split(jnp.concatenate(turned, axis=0))
        flip = (((1,), (1,)), ((), ()))
        wide = dot(outer_table, high, flip)
        outer = wide[:256] + wide[256:] + dot(bh_ref[...], low, flip)
        for i, k in enumerate((k0, k1)):
            for part in range(2):
                images[part][pl.ds(k, 128, stride=8), :] = outer[
                    part * 128 : (part + 1) * 128, i * LANES : (i + 1) * LANES
                ]


def range_transform(parts, cells, tables):
    fixed = lambda *shape: pl.BlockSpec(shape, lambda g: (0,) * len(shape))
    images = pl.pallas_call(
        functools.partial(range_kernel, parts),
        grid=(4,),
        in_specs=[pl.BlockSpec((32, width, 2, 8, LANES), lambda g: (0, 0, 0, g, 0)) for width in parts]
        + [fixed(256, 256), fixed(256, 256), fixed(2, 128, LANES), fixed(256, 256), fixed(256, 256)],
        out_specs=[pl.BlockSpec((1, 128, 8, LANES), lambda g: (g, 0, 0, 0))] * 2,
        out_shape=[jax.ShapeDtypeStruct((4, 128, 8, LANES), F32)] * 2,
        compiler_params=pltpu.CompilerParams(vmem_limit_bytes=40 * 1024 * 1024),
        cost_estimate=pl.CostEstimate(flops=4 * 32 * S * 256 * 3, bytes_accessed=8 * 2**20, transcendentals=0),
        name="range",
    )(*cells, *tables)
    return [image.transpose(0, 2, 1, 3).reshape(32, S) for image in images]


def resampling_weights(interp_tiles, tile_index, tile_count):
    tiles_dev = interp_tiles.shape[0]
    first_block = lax.axis_index("pulse") * tiles_dev
    offsets = tile_index - (first_block + jnp.arange(tiles_dev, dtype=jnp.int32))[:, None]
    live = jnp.arange(SLOTS, dtype=jnp.int32)[None, :] < tile_count[:, None]
    places = jnp.arange(-2, 3, dtype=jnp.int32)
    chosen = ((offsets[:, None, :] == places[None, :, None]) & live[:, None, :]).astype(F32)
    weights = jnp.sum(interp_tiles[:, None] * chosen[:, :, :, None, None], axis=2)
    weights = weights.reshape(tiles_dev, SLOTS, 32, 4, BLOCK).transpose(0, 3, 2, 1, 4)
    weights = weights.reshape(tiles_dev, BLOCK, SLOTS * BLOCK)
    high = lax.reduce_precision(weights, 8, 7)
    return high.astype(BF16), (weights - high).astype(BF16)


def shards(phase_real, phase_imag, interp_tiles, tile_index, tile_count):
    count = lax.axis_size("pulse")
    up = [(i, i + 1) for i in range(count - 1)]
    down = [(i + 1, i) for i in range(count - 1)]
    weights = resampling_weights(interp_tiles, tile_index, tile_count)
    tables = azimuth_tables()
    even = lax.axis_index("pulse") % 2 == 0
    ends = []
    first = 0
    for width in PARTS:
        columns = slice(first * LANES, (first + width) * LANES)
        tail = jnp.stack([phase_real[AZ - HALO :, columns], phase_imag[AZ - HALO :, columns]])
        head = jnp.stack([phase_real[:HALO, columns], phase_imag[:HALO, columns]])
        first += width
        if first < GROUPS:
            phase_real, phase_imag, tail, head = lax.optimization_barrier((phase_real, phase_imag, tail, head))
            ends.append((lax.ppermute(tail, "pulse", up), lax.ppermute(head, "pulse", down)))
            continue
        away = {(a, c): ranks for a, b, c, ranks in RELAYS}
        ways = [
            [(32 * a + r, 32 * b + r) for a, b in pairs for r in range(32) if r not in away.get((a, b), ())]
            for pairs in (up, down)
        ]
        hops = [
            [(32 * legs[k] + r, 32 * legs[k + 1] + r) for *legs, ranks in RELAYS for r in ranks] for k in range(2)
        ]
        both = ("pulse", "range")
        top, bot = lax.ppermute(tail, both, ways[0]), lax.ppermute(head, both, ways[1])
        passed = lax.ppermute(jnp.where(even, head, tail), both, hops[0])
        passed = lax.ppermute(passed, both, hops[1])
        ends.append((jnp.where(even, top + passed, top), jnp.where(even, bot, bot + passed)))
    cells = []
    first = 0
    for width, (top, bot) in zip(PARTS, ends):
        sent = azimuth(first, width, phase_real, phase_imag, top, bot, weights, tables)
        cells.append(lax.all_to_all(sent, "range", split_axis=0, concat_axis=0, tiled=True))
        first += width
    return tuple(range_transform(PARTS, cells, range_tables(PARTS)))


def solution(mesh):
    placed = (
        P("pulse", "range"),
        P("pulse", "range"),
        P("pulse", None, None, None),
        P("pulse", None),
        P("pulse"),
    )
    return jax.shard_map(
        shards,
        mesh=mesh,
        in_specs=placed,
        out_specs=(P(("pulse", "range"), None), P(("pulse", "range"), None)),
        check_vma=False,
    )
```

profile of v0, /device:TPU:1, one launch (start us, length us, event | category | flops | bytes accessed | tf_op | source)
XLA Modules:
  0.0 206.1 jit_solution(17169692293022345424)
XLA Ops:
  0.6 1.1 slice_bitcast_fusion.4
  1.7 1.2 slice_bitcast_fusion.5
  2.9 1.0 pad_maximum_fusion
  4.0 10.5 %collective-permute-start = (f32[2,256,256]{2,1,0:T(8,128)}, f32[2,256,256]{2,1,0:T(8,128)}, u32[]{:S(2)}, u32[]{:S(2)}) collective-permute-start(f32[2,256,256]{2,1,0:T(8,128)} %get-tuple-element.10), channel_id=1, source_target_pairs={{0,32},{32,64},{64,96},{96,128},{128,160},{160,192},{192,224},{1,3... | collective-permute-start | bytes 1572872 | tf_op jit(solution)/shard_map/ppermute | solution.py:237
  14.4 1.3 collective-permute-start.1
  15.7 1.1 slice_bitcast_fusion
  16.9 1.3 pad_maximum_fusion.3
  18.2 1.3 collective-permute-start.5
  19.5 1.3 collective-permute-start.3
  20.8 9.6 %collective-permute-start.2 = (f32[2,256,256]{2,1,0:T(8,128)}, f32[2,256,256]{2,1,0:T(8,128)}, u32[]{:S(2)}, u32[]{:S(2)}) collective-permute-start(f32[2,256,256]{2,1,0:T(8,128)} %get-tuple-element.28), channel_id=1, source_target_pairs={{0,32},{1,33},{2,34},{3,35},{4,36},{5,37},{6,38},{7,39},{8,40},{9,... | collective-permute-start | bytes 1572872 | tf_op jit(solution)/shard_map/ppermute | solution.py:248
  30.4 0.1 iota_compare_fusion
  30.5 0.1 broadcast_subtract_fusion
  30.6 0.1 and_convert_fusion
  30.6 3.5 %multiply_reduce_fusion = f32[8,5,128,128]{3,2,1,0:T(8,128)S(1)} fusion(f32[8,5,5]{2,1,0:T(8,128)S(1)} %and_convert_fusion, f32[8,5,128,128]{3,2,1,0:T(8,128)} %param.15), kind=kLoop, calls=%fused_computation | loop fusion | flops 5898240 | bytes 5243680 | tf_op jit(solution)/shard_map/reduce_sum | solution.py:214
  34.1 1.5 copy.16
  35.6 3.6 %copy.17 = f32[8,4,32,5,128]{4,3,2,1,0:T(8,128)} copy(f32[8,4,32,5,128]{4,0,1,2,3:T(8,128)S(1)} %bitcast.25) | data formatting | bytes 5242880 | tf_op jit(solution)/shard_map/transpose | solution.py:215
  39.2 4.7 %reshape.47 = f32[8,128,640]{2,1,0:T(8,128)} reshape(f32[8,4,32,5,128]{4,3,2,1,0:T(8,128)} %copy.17) | data formatting | bytes 5242880 | tf_op jit(solution)/shard_map/reshape | solution.py:216
  43.9 3.3 %collective-permute-start.4 = (f32[2,256,256]{2,1,0:T(8,128)}, f32[2,256,256]{2,1,0:T(8,128)}, u32[]{:S(2)}, u32[]{:S(2)}) collective-permute-start(f32[2,256,256]{2,1,0:T(8,128)} %collective-permute-done.3), channel_id=1, source_target_pairs={{0,32},{1,33},{2,34},{3,35},{4,36},{5,37},{6,38},{7,39},{8,40},{9,... | collective-permute-start | bytes 1572872 | tf_op jit(solution)/shard_map/ppermute | solution.py:250
  47.2 2.2 %fusion = (bf16[8,128,640]{2,1,0:T(8,128)(2,1)S(1)}, bf16[8,128,640]{2,1,0:T(8,128)(2,1)S(1)}) fusion(f32[8,128,640]{2,1,0:T(8,128)} %reshape.47), kind=kLoop, calls=%fused_computation.3 | loop fusion | flops 2621440 | bytes 5242880 | tf_op jit(solution)/shard_map/convert_element_type | solution.py:218
  49.5 7.0 %azimuth.2 = f32[32,2,2,32,128]{4,3,2,1,0:T(8,128)} custom-call(f32[1024,512]{1,0:T(8,128)S(1)} %copy-done.2, f32[1024,512]{1,0:T(8,128)S(1)} %copy-done.4, f32[2,256,256]{2,1,0:T(8,128)} %collective-permute-done.top_ref, f32[2,256,256]{2,1,0:T(8,128)} %collective-permute-done.1.bot_ref, bf16[8,128,640]{2,1,0:T(8,128)(2,1)S(1)} %get-tuple-element.15.wh_ref, ...), custom_call_target="tpu_custom_call" | custom-call | flops 3623878656 | bytes 4194304 | tf_op jit(solution)/shard_map/azimuth/pallas_call | solution.py:125
  56.5 1.1 copy-done
  57.6 32.2 %all-to-all-start = ((f32[32,2,2,32,128]{4,3,2,1,0:T(8,128)}), f32[32,2,2,32,128]{4,3,2,1,0:T(8,128)}, u32[]{:S(2)}, u32[]{:S(2)}) async-start(f32[32,2,2,32,128]{4,3,2,1,0:T(8,128)} %azimuth.2), calls=%async_computation | async-start | bytes 4194304 | tf_op jit(solution)/shard_map/all_to_all | solution.py:256
  89.8 1.6 add_select_fusion
  91.4 0.1 copy-done.1
  91.5 0.2 copy-done.7
  91.8 0.1 copy-done.11
  91.9 1.6 copy-done.3
  93.5 1.6 copy-done.5
  95.1 5.4 %azimuth.3 = f32[32,2,2,32,128]{4,3,2,1,0:T(8,128)S(1)} custom-call(f32[1024,512]{1,0:T(8,128)S(1)} %copy-done.3, f32[1024,512]{1,0:T(8,128)S(1)} %copy-done.5, f32[2,256,256]{2,1,0:T(8,128)S(1)} %get-tuple-element.25.top_ref, f32[2,256,256]{2,1,0:T(8,128)S(1)} %get-tuple-element.24.bot_ref, bf16[8,128,640]{2,1,0:T(8,128)(2,1)S(1)} %copy-done.1, ...), custom_call_target="tpu_custom_call" | custom-call | flops 362387865600 | bytes 4194304 | tf_op jit(solution)/shard_map/azimuth/pallas_call | solution.py:125
  100.5 40.0 %all-to-all-done.refs_0_ = f32[32,2,2,32,128]{4,3,2,1,0:T(8,128)} async-done(((f32[32,2,2,32,128]{4,3,2,1,0:T(8,128)}), f32[32,2,2,32,128]{4,3,2,1,0:T(8,128)}, u32[]{:S(2)}, u32[]{:S(2)}) %all-to-all-start) | async-done | bytes 2097184 | tf_op jit(solution)/shard_map/all_to_all | solution.py:256
  140.5 57.4 %all_to_all.10.refs_1_ = f32[32,2,2,32,128]{4,3,2,1,0:T(8,128)S(1)} all-to-all(f32[32,2,2,32,128]{4,3,2,1,0:T(8,128)S(1)} %azimuth.3), channel_id=1, replica_groups=mesh['pulse'=8,'range'=32] {'range'}, dimensions={0} | all-to-all | bytes 4194304 | tf_op jit(solution)/shard_map/all_to_all | solution.py:256
  197.9 8.1 %range.1 = (f32[4,128,8,128]{3,2,1,0:T(8,128)}, f32[4,128,8,128]{3,2,1,0:T(8,128)}) custom-call(f32[32,2,2,32,128]{4,3,2,1,0:T(8,128)} %all-to-all-done.refs_0_, f32[32,2,2,32,128]{4,3,2,1,0:T(8,128)S(1)} %all_to_all.10.refs_1_, bf16[256,256]{1,0:T(8,128)(2,1)S(1)} %copy-done.12, bf16[256,256]{1,0:T(8,128)(2,1)S(1)} %copy-done.13, ...), custom_call_target="tpu_custom_call" | custom-call | flops 1610612736 | bytes 8388608 | tf_op jit(solution)/shard_map/range/pallas_call | solution.py:193
  (41 shorter events, 0.2 us)
Async XLA Ops:
  1.7 15.1 %copy-start.2 = (f32[1024,512]{1,0:T(8,128)S(1)}, f32[1024,512]{1,0:T(8,128)}, u32[]{:S(2)}) copy-start(f32[1024,512]{1,0:T(8,128)} %re_ref.1) | copy-start | bytes 6291460
  4.0 45.5 %collective-permute-start = (f32[2,256,256]{2,1,0:T(8,128)}, f32[2,256,256]{2,1,0:T(8,128)}, u32[]{:S(2)}, u32[]{:S(2)}) collective-permute-start(f32[2,256,256]{2,1,0:T(8,128)} %get-tuple-element.10), channel_id=1, source_target_pairs={{0,32},{32,64},{64,96},{96,128},{128,160},{160,192},{192,224},{1,3... | collective-permute-start | bytes 1572872 | tf_op jit(solution)/shard_map/ppermute | solution.py:237
  14.4 35.0 %collective-permute-start.1 = (f32[2,256,256]{2,1,0:T(8,128)}, f32[2,256,256]{2,1,0:T(8,128)}, u32[]{:S(2)}, u32[]{:S(2)}) collective-permute-start(f32[2,256,256]{2,1,0:T(8,128)} %get-tuple-element.11), channel_id=1, source_target_pairs={{32,0},{64,32},{96,64},{128,96},{160,128},{192,160},{224,192},{33,... | collective-permute-start | bytes 1572872 | tf_op jit(solution)/shard_map/ppermute | solution.py:237
  16.8 13.6 %copy-start.18 = (s32[8]{0:T(128)S(1)}, s32[8]{0:T(128)}, u32[]{:S(2)}) copy-start(s32[8]{0:T(128)} %param.17) | copy-start | bytes 100
  16.8 13.7 %copy-start.17 = (s32[8,5]{1,0:T(8,128)S(1)}, s32[8,5]{1,0:T(8,128)}, u32[]{:S(2)}) copy-start(s32[8,5]{1,0:T(8,128)} %param.16) | copy-start | bytes 484
  18.2 71.6 %collective-permute-start.5 = (f32[2,256,256]{2,1,0:T(8,128)}, f32[2,256,256]{2,1,0:T(8,128)}, u32[]{:S(2)}, u32[]{:S(2)}) collective-permute-start(f32[2,256,256]{2,1,0:T(8,128)} %get-tuple-element.26), channel_id=1, source_target_pairs={{32,0},{33,1},{34,2},{35,3},{36,4},{37,5},{38,6},{39,7},{40,8},{41... | collective-permute-start | bytes 1572872 | tf_op jit(solution)/shard_map/ppermute | solution.py:248
  19.5 24.5 %collective-permute-start.3 = (f32[2,256,256]{2,1,0:T(8,128)}, f32[2,256,256]{2,1,0:T(8,128)}, u32[]{:S(2)}, u32[]{:S(2)}) collective-permute-start(f32[2,256,256]{2,1,0:T(8,128)} %get-tuple-element.27), channel_id=1, source_target_pairs={{64,0},{65,1},{66,2},{67,3},{68,4},{69,5},{70,6},{71,7},{72,8},{73... | collective-permute-start | bytes 1572872 | tf_op jit(solution)/shard_map/ppermute | solution.py:249
  20.8 69.0 %collective-permute-start.2 = (f32[2,256,256]{2,1,0:T(8,128)}, f32[2,256,256]{2,1,0:T(8,128)}, u32[]{:S(2)}, u32[]{:S(2)}) collective-permute-start(f32[2,256,256]{2,1,0:T(8,128)} %get-tuple-element.28), channel_id=1, source_target_pairs={{0,32},{1,33},{2,34},{3,35},{4,36},{5,37},{6,38},{7,39},{8,40},{9,... | collective-permute-start | bytes 1572872 | tf_op jit(solution)/shard_map/ppermute | solution.py:248
  43.9 5.5 %copy-start.4 = (f32[1024,512]{1,0:T(8,128)S(1)}, f32[1024,512]{1,0:T(8,128)}, u32[]{:S(2)}) copy-start(f32[1024,512]{1,0:T(8,128)} %im_ref.1) | copy-start | bytes 6291460
  43.9 5.6 %copy-start.6 = (f32[3,2,256,128]{3,2,1,0:T(8,128)S(1)}, f32[3,2,256,128]{3,2,1,0:T(8,128)}, u32[]{:S(2)}) copy-start(f32[3,2,256,128]{3,2,1,0:T(8,128)} %constant.44.clone.tw_ref) | copy-start | bytes 2359300
  43.9 5.6 %copy-start.8 = (bf16[512,256]{1,0:T(8,128)(2,1)S(1)}, bf16[512,256]{1,0:T(8,128)(2,1)}, u32[]{:S(2)}) copy-start(bf16[512,256]{1,0:T(8,128)(2,1)} %constant.42.clone.dh_ref) | copy-start | bytes 786436
  43.9 5.6 %copy-start.10 = (bf16[512,256]{1,0:T(8,128)(2,1)S(1)}, bf16[512,256]{1,0:T(8,128)(2,1)}, u32[]{:S(2)}) copy-start(bf16[512,256]{1,0:T(8,128)(2,1)} %constant.43.clone.dl_ref) | copy-start | bytes 786436
  43.9 45.9 %collective-permute-start.4 = (f32[2,256,256]{2,1,0:T(8,128)}, f32[2,256,256]{2,1,0:T(8,128)}, u32[]{:S(2)}, u32[]{:S(2)}) collective-permute-start(f32[2,256,256]{2,1,0:T(8,128)} %collective-permute-done.3), channel_id=1, source_target_pairs={{0,32},{1,33},{2,34},{3,35},{4,36},{5,37},{6,38},{7,39},{8,40},{9,... | collective-permute-start | bytes 1572872 | tf_op jit(solution)/shard_map/ppermute | solution.py:250
  56.5 1.1 copy-start
  57.6 82.9 %all-to-all-start = ((f32[32,2,2,32,128]{4,3,2,1,0:T(8,128)}), f32[32,2,2,32,128]{4,3,2,1,0:T(8,128)}, u32[]{:S(2)}, u32[]{:S(2)}) async-start(f32[32,2,2,32,128]{4,3,2,1,0:T(8,128)} %azimuth.2), calls=%async_computation | async-start | bytes 4194304 | tf_op jit(solution)/shard_map/all_to_all | solution.py:256
  89.7 1.8 copy-start.1
  89.8 2.0 copy-start.7
  89.8 2.0 copy-start.9
  89.8 2.1 %copy-start.11 = (bf16[512,256]{1,0:T(8,128)(2,1)S(1)}, bf16[512,256]{1,0:T(8,128)(2,1)}, u32[]{:S(2)}) copy-start(bf16[512,256]{1,0:T(8,128)(2,1)} %constant.43.clone.dl_ref) | copy-start | bytes 786436
  91.9 1.6 copy-start.3
  93.5 1.6 copy-start.5
  100.4 97.5 %copy-start.12 = (bf16[256,256]{1,0:T(8,128)(2,1)S(1)}, bf16[256,256]{1,0:T(8,128)(2,1)}, u32[]{:S(2)}) copy-start(bf16[256,256]{1,0:T(8,128)(2,1)} %constant.45.clone.refs_2_) | copy-start | bytes 393220
  100.5 97.5 %copy-start.13 = (bf16[256,256]{1,0:T(8,128)(2,1)S(1)}, bf16[256,256]{1,0:T(8,128)(2,1)}, u32[]{:S(2)}) copy-start(bf16[256,256]{1,0:T(8,128)(2,1)} %constant.46.clone.refs_3_) | copy-start | bytes 393220
  100.5 97.5 %copy-start.14 = (f32[2,128,128]{2,1,0:T(8,128)S(1)}, f32[2,128,128]{2,1,0:T(8,128)}, u32[]{:S(2)}) copy-start(f32[2,128,128]{2,1,0:T(8,128)} %constant.47.clone.refs_4_) | copy-start | bytes 393220
  100.5 97.4 %copy-start.15 = (bf16[256,256]{1,0:T(8,128)(2,1)S(1)}, bf16[256,256]{1,0:T(8,128)(2,1)}, u32[]{:S(2)}) copy-start(bf16[256,256]{1,0:T(8,128)(2,1)} %constant.48.clone.refs_5_) | copy-start | bytes 393220
  100.5 97.4 %copy-start.16 = (bf16[256,256]{1,0:T(8,128)(2,1)S(1)}, bf16[256,256]{1,0:T(8,128)(2,1)}, u32[]{:S(2)}) copy-start(bf16[256,256]{1,0:T(8,128)(2,1)} %constant.49.clone.refs_6_) | copy-start | bytes 393220
where the time goes:
time: 209 us; the launch traced here: 206 us
  starting transfers between devices  59.4 us (28%)
  blocking collectives  57.4 us (27%)
  waiting for transfers between devices  40 us (19%)
  Pallas kernels  20.5 us (10%)
  local copies, waits for them, and re-layouts  17.9 us (9%)
  other arithmetic  9.88 us (5%)
    all_to_all x1, blocking collectives, shards(): lax.all_to_all(sent, 'range', split_axis=0, concat_axis=0, tiled=True)  57.4 us
    all_to_all x1, waiting for transfers between devices, shards(): lax.all_to_all(sent, 'range', split_axis=0, concat_axis=0, tiled=True)  40 us
    all_to_all x1, starting transfers between devices, shards(): lax.all_to_all(sent, 'range', split_axis=0, concat_axis=0, tiled=True)  32.2 us
    pallas_call x2, Pallas kernels, azimuth(): pl.pallas_call(azimuth_kernel, grid=(width,), in_specs=[pl.BlockSpec((AZ,...  12.4 us
    ppermute x1, starting transfers between devices, shards(): lax.ppermute(tail, 'pulse', up)  10.5 us
    ppermute x1, starting transfers between devices, shards(): lax.ppermute(tail, both, ways[0])  9.63 us
    pallas_call x1, Pallas kernels, range_transform(): pl.pallas_call(functools.partial(range_kernel, parts), grid=(4,), in_spec...  8.14 us
    unnamed x38, local copies, waits for them, and re-layouts  4.75 us
  transfers between devices with their start and end apart: 7, of which 1 were waited for; matrix products, arithmetic and copies ran while one was open for 10% of the time, Pallas kernels for 6%

commit v1 on v0

--- a/solution.py
+++ b/solution.py
@@ -20,12 +20,13 @@
 GROUPS = 4
 ALL = tuple(range(32))
 ONE_CORE = tuple(range(0, 32, 2))
+MOST = tuple(r for r in range(32) if r % 2 == 0 or r // 8 in (1, 2))
 MIDDLE = tuple(r for r in ONE_CORE if r // 8 in (1, 2))
 RELAYS = (
     (2, 0, 1, ALL),
     (5, 7, 6, ALL),
-    (3, 5, 4, ONE_CORE),
-    (4, 2, 3, ONE_CORE),
+    (3, 5, 4, MOST),
+    (4, 2, 3, MOST),
     (1, 3, 2, MIDDLE),
     (6, 4, 5, MIDDLE),
 )
@@ -81,26 +82,56 @@
     return lax.dot_general(a, b, dims, preferred_element_type=F32)
 
 
-def azimuth_kernel(re_ref, im_ref, top_ref, bot_ref, wh_ref, wl_ref, dh_ref, dl_ref, tw_ref, out_ref, xh, xl, yh, yl):
-    def put(row, real, imag):
-        high, low = split(jnp.concatenate([real, imag], axis=1))
-        xh[row : row + BLOCK, :] = high
-        xl[row : row + BLOCK, :] = low
-
-    for i in range(2):
-        rows = slice(i * BLOCK, (i + 1) * BLOCK)
-        put(i * BLOCK, top_ref[0, rows], top_ref[1, rows])
-        put(HALO + AZ + i * BLOCK, bot_ref[0, rows], bot_ref[1, rows])
+def own_kernel(re_ref, im_ref, wh_ref, wl_ref, out_ref, xh, xl):
     for i in range(AZ // BLOCK):
         rows = slice(i * BLOCK, (i + 1) * BLOCK)
-        put(HALO + i * BLOCK, re_ref[rows], im_ref[rows])
+        xh[rows], xl[rows] = split(jnp.concatenate([re_ref[rows], im_ref[rows]], axis=1))
     for b in range(AZ // BLOCK):
-        rows = slice(b * BLOCK, (b + SLOTS) * BLOCK)
-        cells = dot(wh_ref[b], xh[rows]) + dot(wl_ref[b], xh[rows]) + dot(wh_ref[b], xl[rows])
+        low, high = max(b - 2, 0), min(b + 3, AZ // BLOCK)
+        rows = slice(low * BLOCK, high * BLOCK)
+        slots = slice((low - b + 2) * BLOCK, (high - b + 2) * BLOCK)
+        wh, wl = wh_ref[b, :, slots], wl_ref[b, :, slots]
+        out_ref[0, b * BLOCK : (b + 1) * BLOCK] = dot(wh, xh[rows]) + dot(wl, xh[rows]) + dot(wh, xl[rows])
+
+
+def own_part(phase_real, phase_imag, weights):
+    tile = pl.BlockSpec((8, BLOCK, SLOTS * BLOCK), lambda i: (0, 0, 0))
+    return pl.pallas_call(
+        own_kernel,
+        grid=(GROUPS,),
+        in_specs=[pl.BlockSpec((AZ, LANES), lambda i: (0, i))] * 2 + [tile, tile],
+        out_specs=pl.BlockSpec((1, AZ, 2 * LANES), lambda i: (i, 0, 0)),
+        out_shape=jax.ShapeDtypeStruct((GROUPS, AZ, 2 * LANES), F32),
+        scratch_shapes=[pltpu.VMEM((AZ, 2 * LANES), BF16)] * 2,
+        compiler_params=pltpu.CompilerParams(vmem_limit_bytes=40 * 1024 * 1024),
+        cost_estimate=pl.CostEstimate(flops=1, bytes_accessed=1, transcendentals=0),
+        name="own",
+    )(phase_real, phase_imag, *weights)
+
+
+def edge_weights(weights):
+    none = jnp.zeros((BLOCK, BLOCK), weights.dtype)
+    before = [weights[0, :, : 2 * BLOCK], jnp.concatenate([none, weights[1, :, :BLOCK]], axis=1)]
+    after = [jnp.concatenate([weights[6, :, 4 * BLOCK :], none], axis=1), weights[7, :, 3 * BLOCK :]]
+    return jnp.stack([jnp.concatenate(before, axis=0), jnp.concatenate(after, axis=0)])
+
+
+def azimuth_kernel(own_ref, top_ref, bot_ref, wh_ref, wl_ref, dh_ref, dl_ref, tw_ref, out_ref, yh, yl):
+    def put(row, cells):
         high, low = split(cells)
-        for a in range(4):
-            yh[a, b * 32 : (b + 1) * 32] = high[a * 32 : (a + 1) * 32]
-            yl[a, b * 32 : (b + 1) * 32] = low[a * 32 : (a + 1) * 32]
+        for b in range(2):
+            for a in range(4):
+                rows = slice(b * BLOCK + a * 32, b * BLOCK + (a + 1) * 32)
+                place = row // 4 + b * 32
+                yh[a, place : place + 32] = high[rows]
+                yl[a, place : place + 32] = low[rows]
+
+    for side, (row, ref) in enumerate(((0, top_ref), (AZ - HALO, bot_ref))):
+        high, low = split(jnp.concatenate([ref[0], ref[1]], axis=1))
+        wh, wl = wh_ref[side], wl_ref[side]
+        put(row, own_ref[0, row : row + HALO] + (dot(wh, high) + dot(wl, high) + dot(wh, low)))
+    for row in range(HALO, AZ - HALO, HALO):
+        put(row, own_ref[0, row : row + HALO])
     real, imag = [], []
     for a in range(4):
         four = dot(dh_ref[...], yh[a]) + dot(dl_ref[...], yh[a]) + dot(dh_ref[...], yl[a])
@@ -120,36 +151,30 @@
                 out_ref[quarter * 8 + t, 0, part] = bins[quarter][part][t * 32 : (t + 1) * 32]
 
 
-def azimuth(first, width, phase_real, phase_imag, top, bot, weights, tables):
+def azimuth(first, width, own, top, bot, weights, tables):
     fixed = lambda *shape: pl.BlockSpec(shape, lambda i: (0,) * len(shape))
     return pl.pallas_call(
         azimuth_kernel,
         grid=(width,),
         in_specs=[
-            pl.BlockSpec((AZ, LANES), lambda i: (0, first + i)),
-            pl.BlockSpec((AZ, LANES), lambda i: (0, first + i)),
+            pl.BlockSpec((1, AZ, 2 * LANES), lambda i: (first + i, 0, 0)),
             pl.BlockSpec((2, HALO, LANES), lambda i: (0, 0, i)),
             pl.BlockSpec((2, HALO, LANES), lambda i: (0, 0, i)),
-            fixed(8, BLOCK, SLOTS * BLOCK),
-            fixed(8, BLOCK, SLOTS * BLOCK),
+            fixed(2, HALO, HALO),
+            fixed(2, HALO, HALO),
             fixed(512, 256),
             fixed(512, 256),
             fixed(3, 2, 256, LANES),
         ],
         out_specs=pl.BlockSpec((32, 1, 2, 32, LANES), lambda i: (0, i, 0, 0, 0)),
         out_shape=jax.ShapeDtypeStruct((32, width, 2, 32, LANES), F32),
-        scratch_shapes=[
-            pltpu.VMEM((AZ + 2 * HALO, 2 * LANES), BF16),
-            pltpu.VMEM((AZ + 2 * HALO, 2 * LANES), BF16),
-            pltpu.VMEM((4, 256, 2 * LANES), BF16),
-            pltpu.VMEM((4, 256, 2 * LANES), BF16),
-        ],
+        scratch_shapes=[pltpu.VMEM((4, 256, 2 * LANES), BF16)] * 2,
         compiler_params=pltpu.CompilerParams(vmem_limit_bytes=40 * 1024 * 1024),
         cost_estimate=pl.CostEstimate(
-            flops=6 * width * 256 * (AZ * 640 + AZ * 512) * (100 if first else 1), bytes_accessed=width * 2 * 2**20, transcendentals=0
+            flops=6 * width * 256 * AZ * 1152 * (100 if first else 1), bytes_accessed=width * 2**21, transcendentals=0
         ),
         name="azimuth",
-    )(phase_real, phase_imag, top, bot, *weights, *tables)
+    )(own, top, bot, *weights, *tables)
 
 
 def range_kernel(parts, *refs):
@@ -236,6 +261,7 @@
             phase_real, phase_imag, tail, head = lax.optimization_barrier((phase_real, phase_imag, tail, head))
             ends.append((lax.ppermute(tail, "pulse", up), lax.ppermute(head, "pulse", down)))
             continue
+        tail, head, *weights = lax.optimization_barrier((tail, head, *weights))
         away = {(a, c): ranks for a, b, c, ranks in RELAYS}
         ways = [
             [(32 * a + r, 32 * b + r) for a, b in pairs for r in range(32) if r not in away.get((a, b), ())]
@@ -249,10 +275,12 @@
         passed = lax.ppermute(jnp.where(even, head, tail), both, hops[0])
         passed = lax.ppermute(passed, both, hops[1])
         ends.append((jnp.where(even, top + passed, top), jnp.where(even, bot, bot + passed)))
+    own = own_part(phase_real, phase_imag, weights)
+    edges = [edge_weights(half) for half in weights]
     cells = []
     first = 0
     for width, (top, bot) in zip(PARTS, ends):
-        sent = azimuth(first, width, phase_real, phase_imag, top, bot, weights, tables)
+        sent = azimuth(first, width, own, top, bot, edges, tables)
         cells.append(lax.all_to_all(sent, "range", split_axis=0, concat_axis=0, tiled=True))
         first += width
     return tuple(range_transform(PARTS, cells, range_tables(PARTS)))

time: 209 us -> 209 us (level)
  starting transfers between devices: 59.4 us -> 39.9 us
  waiting for transfers between devices: 40 us -> 56.7 us
  local copies, waits for them, and re-layouts: 17.9 us -> 21.5 us
    all_to_all x1, starting transfers between devices: 32.2 us -> 14.1 us  [shards(): lax.all_to_all(sent, 'range', split_axis=0, concat_axis=0, tiled=True)]
    ppermute x1, waiting for transfers between devices: 0.01 us -> 9.41 us  [shards(): lax.ppermute(head, both, ways[1])]
    ppermute x1, waiting for transfers between devices: 0.01 us -> 5.46 us  [shards(): passed = lax.ppermute(jnp.where(even, head, tail), both, hops[0])]
    another operation x4, local copies, waits for them, and re-layouts: 3.38 us -> 5.82 us  [shards(): head = jnp.stack([phase_real[:HALO, columns], phase_imag[:HALO, columns]])]
    reduce_sum x1, other arithmetic: 3.49 us -> 1.38 us  [resampling_weights(): jnp.sum(interp_tiles[:, None] * chosen[:, :, :, None, None], axis=2)]
    unnamed x38 -> x40, local copies, waits for them, and re-layouts: 4.75 us -> 5.83 us
    pallas_call x2 -> x3, Pallas kernels: 12.4 us -> 13.3 us  [the longest x2 7.97 us: azimuth(): pl.pallas_call(azimuth_kernel, grid=(width,), in_specs=[pl.BlockSpec((1,...]
  transfers between devices with their start and end apart: 7 -> 7, of which waited for: 1 -> 3; matrix products, arithmetic and copies ran while one was open for 10% -> 10% of each run, Pallas kernels for 6% -> 6%
where the time goes in v1:
time: 209 us; the launch traced here: 208 us
  blocking collectives  57.7 us (28%)
  waiting for transfers between devices  56.7 us (27%)
  starting transfers between devices  39.9 us (19%)
  local copies, waits for them, and re-layouts  21.5 us (10%)
  Pallas kernels  21.5 us (10%)
  other arithmetic  9.32 us (4%)
    all_to_all x1, blocking collectives, shards(): lax.all_to_all(sent, 'range', split_axis=0, concat_axis=0, tiled=True)  57.7 us
    all_to_all x1, waiting for transfers between devices, shards(): lax.all_to_all(sent, 'range', split_axis=0, concat_axis=0, tiled=True)  41.8 us
    all_to_all x1, starting transfers between devices, shards(): lax.all_to_all(sent, 'range', split_axis=0, concat_axis=0, tiled=True)  14.1 us
    ppermute x1, starting transfers between devices, shards(): lax.ppermute(tail, 'pulse', up)  9.79 us
    ppermute x1, waiting for transfers between devices, shards(): lax.ppermute(head, both, ways[1])  9.41 us
    ppermute x1, starting transfers between devices, shards(): lax.ppermute(tail, both, ways[0])  8.73 us
    pallas_call x1, Pallas kernels, range_transform(): pl.pallas_call(functools.partial(range_kernel, parts), grid=(4,), in_spec...  8.14 us
    pallas_call x2, Pallas kernels, azimuth(): pl.pallas_call(azimuth_kernel, grid=(width,), in_specs=[pl.BlockSpec((1,...  7.97 us
  transfers between devices with their start and end apart: 7, of which 3 were waited for; matrix products, arithmetic and copies ran while one was open for 10% of the time, Pallas kernels for 6%

profile of v1, /device:TPU:1, one launch (start us, length us, event | category | flops | bytes accessed | tf_op | source)
XLA Modules:
  0.0 207.7 jit_solution(6173570520946132758)
XLA Ops:
  0.6 1.1 slice_bitcast_fusion.5
  1.7 1.1 slice_bitcast_fusion.4
  2.8 1.0 pad_maximum_fusion
  3.8 9.8 %collective-permute-start = (f32[2,256,256]{2,1,0:T(8,128)}, f32[2,256,256]{2,1,0:T(8,128)S(1)}, u32[]{:S(2)}, u32[]{:S(2)}) collective-permute-start(f32[2,256,256]{2,1,0:T(8,128)} %get-tuple-element.16), channel_id=1, source_target_pairs={{0,32},{32,64},{64,96},{96,128},{128,160},{160,192},{192,224},{1,3... | collective-permute-start | bytes 1572872 | tf_op jit(solution)/shard_map/ppermute | solution.py:262
  13.6 1.3 collective-permute-start.1
  15.1 1.8 slice_bitcast_fusion.1
  16.8 1.9 slice_bitcast_fusion
  18.9 1.4 multiply_reduce_fusion
  20.3 1.5 copy.16
  21.8 3.6 %copy.17 = f32[8,4,32,5,128]{4,3,2,1,0:T(8,128)} copy(f32[8,4,32,5,128]{4,0,1,2,3:T(8,128)S(1)} %bitcast.49) | data formatting | bytes 5242880 | tf_op jit(solution)/shard_map/transpose | solution.py:240
  25.4 4.7 %reshape.47 = f32[8,128,640]{2,1,0:T(8,128)} reshape(f32[8,4,32,5,128]{4,3,2,1,0:T(8,128)} %copy.17) | data formatting | bytes 5242880 | tf_op jit(solution)/shard_map/reshape | solution.py:241
  30.1 2.3 %fusion = (bf16[8,128,640]{2,1,0:T(8,128)(2,1)S(1)}, bf16[8,128,640]{2,1,0:T(8,128)(2,1)S(1)}) fusion(f32[8,128,640]{2,1,0:T(8,128)} %reshape.47), kind=kLoop, calls=%fused_computation.3 | loop fusion | flops 2621440 | bytes 5242880 | tf_op jit(solution)/shard_map/convert_element_type | solution.py:243
  32.4 0.8 pad_maximum_fusion.3
  33.3 0.9 pad_maximum_fusion.2
  34.1 8.7 %collective-permute-start.2 = (f32[2,256,256]{2,1,0:T(8,128)}, f32[2,256,256]{2,1,0:T(8,128)}, u32[]{:S(2)}, u32[]{:S(2)}) collective-permute-start(f32[2,256,256]{2,1,0:T(8,128)} %pad_maximum_fusion.2), channel_id=1, source_target_pairs={{0,32},{1,33},{2,34},{3,35},{4,36},{5,37},{6,38},{7,39},{8,40},{9,... | collective-permute-start | bytes 1572872 | tf_op jit(solution)/shard_map/ppermute | solution.py:274
  42.9 1.3 collective-permute-start.5
  44.2 1.3 broadcast_select_fusion
  45.4 1.3 collective-permute-start.3
  46.9 1.6 copy-done.1
  48.5 5.4 %own.1.own_ref = f32[4,1024,256]{2,1,0:T(8,128)S(1)} custom-call(f32[1024,512]{1,0:T(8,128)S(1)} %copy-done, f32[1024,512]{1,0:T(8,128)S(1)} %copy-done.1, bf16[8,128,640]{2,1,0:T(8,128)(2,1)S(1)} %get-tuple-element.14.wh_ref, bf16[8,128,640]{2,1,0:T(8,128)(2,1)S(1)} %get-tuple-element.15.wl_ref), custom_call_target="tpu_custom_call" | custom-call | flops 1 | bytes 1 | tf_op jit(solution)/shard_map/own/pallas_call | solution.py:99
  53.9 5.5 %collective-permute-done.3 = f32[2,256,256]{2,1,0:T(8,128)} collective-permute-done((f32[2,256,256]{2,1,0:T(8,128)S(1)}, f32[2,256,256]{2,1,0:T(8,128)}, u32[]{:S(2)}, u32[]{:S(2)}) %collective-permute-start.3) | collective-permute-done | bytes 524320 | tf_op jit(solution)/shard_map/ppermute | solution.py:275
  59.3 3.4 %collective-permute-start.4 = (f32[2,256,256]{2,1,0:T(8,128)}, f32[2,256,256]{2,1,0:T(8,128)S(1)}, u32[]{:S(2)}, u32[]{:S(2)}) collective-permute-start(f32[2,256,256]{2,1,0:T(8,128)} %collective-permute-done.3), channel_id=1, source_target_pairs={{0,32},{1,33},{2,34},{3,35},{4,36},{5,37},{6,38},{7,39},{8,40},{9,... | collective-permute-start | bytes 1572872 | tf_op jit(solution)/shard_map/ppermute | solution.py:276
  62.9 4.8 %azimuth.2 = f32[32,2,2,32,128]{4,3,2,1,0:T(8,128)} custom-call(f32[4,1024,256]{2,1,0:T(8,128)S(1)} %own.1.own_ref, f32[2,256,256]{2,1,0:T(8,128)S(1)} %collective-permute-done.top_ref, f32[2,256,256]{2,1,0:T(8,128)} %collective-permute-done.1.bot_ref, bf16[2,256,256]{2,1,0:T(8,128)(2,1)S(1)} %pad_maximum_fusion.4.wh_ref, ...), custom_call_target="tpu_custom_call" | custom-call | flops 3623878656 | bytes 4194304 | tf_op jit(solution)/shard_map/azimuth/pallas_call | solution.py:156
  67.7 2.0 copy-done.2
  69.7 14.1 %all-to-all-start = ((f32[32,2,2,32,128]{4,3,2,1,0:T(8,128)}), f32[32,2,2,32,128]{4,3,2,1,0:T(8,128)}, u32[]{:S(2)}, u32[]{:S(2)}) async-start(f32[32,2,2,32,128]{4,3,2,1,0:T(8,128)} %azimuth.2), calls=%async_computation | async-start | bytes 4194304 | tf_op jit(solution)/shard_map/all_to_all | solution.py:284
  83.9 9.4 %collective-permute-done.5 = f32[2,256,256]{2,1,0:T(8,128)} collective-permute-done((f32[2,256,256]{2,1,0:T(8,128)}, f32[2,256,256]{2,1,0:T(8,128)}, u32[]{:S(2)}, u32[]{:S(2)}) %collective-permute-start.5) | collective-permute-done | bytes 524320 | tf_op jit(solution)/shard_map/ppermute | solution.py:274
  93.3 1.3 add_select_fusion
  94.6 2.2 %copy-done.3 = f32[4,1024,256]{2,1,0:T(8,128)S(1)} copy-done((f32[4,1024,256]{2,1,0:T(8,128)S(1)}, f32[4,1024,256]{2,1,0:T(8,128)}, u32[]{:S(2)}) %copy-start.3) | copy-done | bytes 4194328
  96.8 3.1 %azimuth.3 = f32[32,2,2,32,128]{4,3,2,1,0:T(8,128)S(1)} custom-call(f32[4,1024,256]{2,1,0:T(8,128)S(1)} %copy-done.3, f32[2,256,256]{2,1,0:T(8,128)S(1)} %get-tuple-element.41.top_ref, f32[2,256,256]{2,1,0:T(8,128)S(1)} %get-tuple-element.40.bot_ref, bf16[2,256,256]{2,1,0:T(8,128)(2,1)S(1)} %pad_maximum_fusion.4.wh_ref, ...), custom_call_target="tpu_custom_call" | custom-call | flops 362387865600 | bytes 4194304 | tf_op jit(solution)/shard_map/azimuth/pallas_call | solution.py:156
  100.0 41.8 %all-to-all-done.refs_0_ = f32[32,2,2,32,128]{4,3,2,1,0:T(8,128)} async-done(((f32[32,2,2,32,128]{4,3,2,1,0:T(8,128)}), f32[32,2,2,32,128]{4,3,2,1,0:T(8,128)}, u32[]{:S(2)}, u32[]{:S(2)}) %all-to-all-start) | async-done | bytes 2097184 | tf_op jit(solution)/shard_map/all_to_all | solution.py:284
  141.8 57.7 %all_to_all.10.refs_1_ = f32[32,2,2,32,128]{4,3,2,1,0:T(8,128)S(1)} all-to-all(f32[32,2,2,32,128]{4,3,2,1,0:T(8,128)S(1)} %azimuth.3), channel_id=1, replica_groups=mesh['pulse'=8,'range'=32] {'range'}, dimensions={0} | all-to-all | bytes 4194304 | tf_op jit(solution)/shard_map/all_to_all | solution.py:284
  199.6 8.1 %range.1 = (f32[4,128,8,128]{3,2,1,0:T(8,128)}, f32[4,128,8,128]{3,2,1,0:T(8,128)}) custom-call(f32[32,2,2,32,128]{4,3,2,1,0:T(8,128)} %all-to-all-done.refs_0_, f32[32,2,2,32,128]{4,3,2,1,0:T(8,128)S(1)} %all_to_all.10.refs_1_, bf16[256,256]{1,0:T(8,128)(2,1)S(1)} %copy-done.13, bf16[256,256]{1,0:T(8,128)(2,1)S(1)} %copy-done.12, ...), custom_call_target="tpu_custom_call" | custom-call | flops 1610612736 | bytes 8388608 | tf_op jit(solution)/shard_map/range/pallas_call | solution.py:218
  (56 shorter events, 0.5 us)
Async XLA Ops:
  0.6 14.3 %copy-start.19 = (s32[8]{0:T(128)S(1)}, s32[8]{0:T(128)}, u32[]{:S(2)}) copy-start(s32[8]{0:T(128)} %param.17) | copy-start | bytes 100
  2.8 16.0 %copy-start.18 = (s32[8,5]{1,0:T(8,128)S(1)}, s32[8,5]{1,0:T(8,128)}, u32[]{:S(2)}) copy-start(s32[8,5]{1,0:T(8,128)} %param.16) | copy-start | bytes 484
  2.8 16.1 %copy-start.14 = (f32[8,5,128,128]{3,2,1,0:T(8,128)S(1)}, f32[8,5,128,128]{3,2,1,0:T(8,128)}, u32[]{:S(2)}) copy-start(f32[8,5,128,128]{3,2,1,0:T(8,128)} %param.15) | copy-start | bytes 7864324
  3.8 59.0 %collective-permute-start = (f32[2,256,256]{2,1,0:T(8,128)}, f32[2,256,256]{2,1,0:T(8,128)S(1)}, u32[]{:S(2)}, u32[]{:S(2)}) collective-permute-start(f32[2,256,256]{2,1,0:T(8,128)} %get-tuple-element.16), channel_id=1, source_target_pairs={{0,32},{32,64},{64,96},{96,128},{128,160},{160,192},{192,224},{1,3... | collective-permute-start | bytes 1572872 | tf_op jit(solution)/shard_map/ppermute | solution.py:262
  13.6 49.2 %collective-permute-start.1 = (f32[2,256,256]{2,1,0:T(8,128)}, f32[2,256,256]{2,1,0:T(8,128)}, u32[]{:S(2)}, u32[]{:S(2)}) collective-permute-start(f32[2,256,256]{2,1,0:T(8,128)} %get-tuple-element.17), channel_id=1, source_target_pairs={{32,0},{64,32},{96,64},{128,96},{160,128},{192,160},{224,192},{33,... | collective-permute-start | bytes 1572872 | tf_op jit(solution)/shard_map/ppermute | solution.py:262
  30.1 2.3 %copy-start.16 = (f32[1,256,256]{2,1,0:T(8,128)S(1)}, f32[1,256,256]{2,1,0:T(8,128)}, u32[]{:S(2)}) copy-start(f32[1,256,256]{2,1,0:T(8,128)} %get-tuple-element.24) | copy-start | bytes 786436
  30.1 2.3 %copy-start.17 = (f32[1,256,256]{2,1,0:T(8,128)S(1)}, f32[1,256,256]{2,1,0:T(8,128)}, u32[]{:S(2)}) copy-start(f32[1,256,256]{2,1,0:T(8,128)} %get-tuple-element.26) | copy-start | bytes 786436
  30.1 3.2 %copy-start.15 = (f32[1,256,256]{2,1,0:T(8,128)S(1)}, f32[1,256,256]{2,1,0:T(8,128)}, u32[]{:S(2)}) copy-start(f32[1,256,256]{2,1,0:T(8,128)} %get-tuple-element.27) | copy-start | bytes 786436
  34.1 49.7 %collective-permute-start.2 = (f32[2,256,256]{2,1,0:T(8,128)}, f32[2,256,256]{2,1,0:T(8,128)}, u32[]{:S(2)}, u32[]{:S(2)}) collective-permute-start(f32[2,256,256]{2,1,0:T(8,128)} %pad_maximum_fusion.2), channel_id=1, source_target_pairs={{0,32},{1,33},{2,34},{3,35},{4,36},{5,37},{6,38},{7,39},{8,40},{9,... | collective-permute-start | bytes 1572872 | tf_op jit(solution)/shard_map/ppermute | solution.py:274
  42.9 50.4 %collective-permute-start.5 = (f32[2,256,256]{2,1,0:T(8,128)}, f32[2,256,256]{2,1,0:T(8,128)}, u32[]{:S(2)}, u32[]{:S(2)}) collective-permute-start(f32[2,256,256]{2,1,0:T(8,128)} %pad_maximum_fusion.3), channel_id=1, source_target_pairs={{32,0},{33,1},{34,2},{35,3},{36,4},{37,5},{38,6},{39,7},{40,8},{41... | collective-permute-start | bytes 1572872 | tf_op jit(solution)/shard_map/ppermute | solution.py:274
  44.2 2.7 %copy-start = (f32[1024,512]{1,0:T(8,128)S(1)}, f32[1024,512]{1,0:T(8,128)}, u32[]{:S(2)}) copy-start(f32[1024,512]{1,0:T(8,128)} %re_ref) | copy-start | bytes 6291460
  45.4 13.9 %collective-permute-start.3 = (f32[2,256,256]{2,1,0:T(8,128)S(1)}, f32[2,256,256]{2,1,0:T(8,128)}, u32[]{:S(2)}, u32[]{:S(2)}) collective-permute-start(f32[2,256,256]{2,1,0:T(8,128)S(1)} %broadcast_select_fusion), channel_id=1, source_target_pairs={{64,0},{65,1},{66,2},{67,3},{68,4},{69,5},{70,6},{71,7},{72,8},{73... | collective-permute-start | bytes 1572872 | tf_op jit(solution)/shard_map/ppermute | solution.py:275
  46.9 1.6 copy-start.1
  48.5 14.4 %copy-start.4 = (f32[3,2,256,128]{3,2,1,0:T(8,128)S(1)}, f32[3,2,256,128]{3,2,1,0:T(8,128)}, u32[]{:S(2)}) copy-start(f32[3,2,256,128]{3,2,1,0:T(8,128)} %constant.46.clone.tw_ref) | copy-start | bytes 2359300
  48.5 14.4 %copy-start.6 = (bf16[512,256]{1,0:T(8,128)(2,1)S(1)}, bf16[512,256]{1,0:T(8,128)(2,1)}, u32[]{:S(2)}) copy-start(bf16[512,256]{1,0:T(8,128)(2,1)} %constant.45.clone.dl_ref) | copy-start | bytes 786436
  48.5 14.4 %copy-start.7 = (bf16[512,256]{1,0:T(8,128)(2,1)S(1)}, bf16[512,256]{1,0:T(8,128)(2,1)}, u32[]{:S(2)}) copy-start(bf16[512,256]{1,0:T(8,128)(2,1)} %constant.44.clone.dh_ref) | copy-start | bytes 786436
  59.3 33.9 %collective-permute-start.4 = (f32[2,256,256]{2,1,0:T(8,128)}, f32[2,256,256]{2,1,0:T(8,128)S(1)}, u32[]{:S(2)}, u32[]{:S(2)}) collective-permute-start(f32[2,256,256]{2,1,0:T(8,128)} %collective-permute-done.3), channel_id=1, source_target_pairs={{0,32},{1,33},{2,34},{3,35},{4,36},{5,37},{6,38},{7,39},{8,40},{9,... | collective-permute-start | bytes 1572872 | tf_op jit(solution)/shard_map/ppermute | solution.py:276
  67.7 2.0 copy-start.2
  69.7 72.1 %all-to-all-start = ((f32[32,2,2,32,128]{4,3,2,1,0:T(8,128)}), f32[32,2,2,32,128]{4,3,2,1,0:T(8,128)}, u32[]{:S(2)}, u32[]{:S(2)}) async-start(f32[32,2,2,32,128]{4,3,2,1,0:T(8,128)} %azimuth.2), calls=%async_computation | async-start | bytes 4194304 | tf_op jit(solution)/shard_map/all_to_all | solution.py:284
  83.8 10.8 %copy-start.5 = (f32[3,2,256,128]{3,2,1,0:T(8,128)S(1)}, f32[3,2,256,128]{3,2,1,0:T(8,128)}, u32[]{:S(2)}) copy-start(f32[3,2,256,128]{3,2,1,0:T(8,128)} %constant.46.clone.tw_ref) | copy-start | bytes 2359300
  83.8 10.8 %copy-start.8 = (bf16[512,256]{1,0:T(8,128)(2,1)S(1)}, bf16[512,256]{1,0:T(8,128)(2,1)}, u32[]{:S(2)}) copy-start(bf16[512,256]{1,0:T(8,128)(2,1)} %constant.44.clone.dh_ref) | copy-start | bytes 786436
  94.6 2.2 %copy-start.3 = (f32[4,1024,256]{2,1,0:T(8,128)S(1)}, f32[4,1024,256]{2,1,0:T(8,128)}, u32[]{:S(2)}) copy-start(f32[4,1024,256]{2,1,0:T(8,128)} %copy-done.2) | copy-start | bytes 12582916
  99.9 99.6 %copy-start.9 = (bf16[256,256]{1,0:T(8,128)(2,1)S(1)}, bf16[256,256]{1,0:T(8,128)(2,1)}, u32[]{:S(2)}) copy-start(bf16[256,256]{1,0:T(8,128)(2,1)} %constant.51.clone.refs_6_) | copy-start | bytes 393220
  99.9 99.6 %copy-start.10 = (bf16[256,256]{1,0:T(8,128)(2,1)S(1)}, bf16[256,256]{1,0:T(8,128)(2,1)}, u32[]{:S(2)}) copy-start(bf16[256,256]{1,0:T(8,128)(2,1)} %constant.50.clone.refs_5_) | copy-start | bytes 393220
  100.0 99.6 %copy-start.11 = (f32[2,128,128]{2,1,0:T(8,128)S(1)}, f32[2,128,128]{2,1,0:T(8,128)}, u32[]{:S(2)}) copy-start(f32[2,128,128]{2,1,0:T(8,128)} %constant.49.clone.refs_4_) | copy-start | bytes 393220
  100.0 99.6 %copy-start.12 = (bf16[256,256]{1,0:T(8,128)(2,1)S(1)}, bf16[256,256]{1,0:T(8,128)(2,1)}, u32[]{:S(2)}) copy-start(bf16[256,256]{1,0:T(8,128)(2,1)} %constant.48.clone.refs_3_) | copy-start | bytes 393220
  100.0 99.6 %copy-start.13 = (bf16[256,256]{1,0:T(8,128)(2,1)S(1)}, bf16[256,256]{1,0:T(8,128)(2,1)}, u32[]{:S(2)}) copy-start(bf16[256,256]{1,0:T(8,128)(2,1)} %constant.47.clone.refs_2_) | copy-start | bytes 393220

commit v2 on v1

--- a/solution.py
+++ b/solution.py
@@ -20,7 +20,7 @@
 GROUPS = 4
 ALL = tuple(range(32))
 ONE_CORE = tuple(range(0, 32, 2))
-MOST = tuple(r for r in range(32) if r % 2 == 0 or r // 8 in (1, 2))
+MOST = tuple(r for r in range(32) if r % 2 == 0 or r // 8 == 1 + r // 2 % 2)
 MIDDLE = tuple(r for r in ONE_CORE if r // 8 in (1, 2))
 RELAYS = (
     (2, 0, 1, ALL),
@@ -229,6 +229,26 @@
     return [image.transpose(0, 2, 1, 3).reshape(32, S) for image in images]
 
 
+def ends_kernel(real_tail, imag_tail, real_head, imag_head, tail_ref, head_ref):
+    for out_ref, parts in ((tail_ref, (real_tail, imag_tail)), (head_ref, (real_head, imag_head))):
+        for part, ref in enumerate(parts):
+            out_ref[part] = ref[...]
+
+
+def block_ends(chunk, phase_real, phase_imag):
+    block = lambda rows: pl.BlockSpec((HALO, 2 * LANES), lambda i: (rows, chunk))
+    return pl.pallas_call(
+        ends_kernel,
+        grid=(1,),
+        in_specs=[block(AZ // HALO - 1)] * 2 + [block(0)] * 2,
+        out_specs=[pl.BlockSpec((2, HALO, 2 * LANES), lambda i: (0, 0, 0))] * 2,
+        out_shape=[jax.ShapeDtypeStruct((2, HALO, 2 * LANES), F32)] * 2,
+        compiler_params=pltpu.CompilerParams(vmem_limit_bytes=60 * 1024 * 1024),
+        cost_estimate=pl.CostEstimate(flops=0, bytes_accessed=2 * 2**20, transcendentals=0),
+        name="ends",
+    )(phase_real, phase_imag, phase_real, phase_imag)
+
+
 def resampling_weights(interp_tiles, tile_index, tile_count):
     tiles_dev = interp_tiles.shape[0]
     first_block = lax.axis_index("pulse") * tiles_dev
@@ -253,15 +273,12 @@
     ends = []
     first = 0
     for width in PARTS:
-        columns = slice(first * LANES, (first + width) * LANES)
-        tail = jnp.stack([phase_real[AZ - HALO :, columns], phase_imag[AZ - HALO :, columns]])
-        head = jnp.stack([phase_real[:HALO, columns], phase_imag[:HALO, columns]])
+        tail, head = block_ends(first // width, phase_real, phase_imag)
         first += width
         if first < GROUPS:
             phase_real, phase_imag, tail, head = lax.optimization_barrier((phase_real, phase_imag, tail, head))
             ends.append((lax.ppermute(tail, "pulse", up), lax.ppermute(head, "pulse", down)))
             continue
-        tail, head, *weights = lax.optimization_barrier((tail, head, *weights))
         away = {(a, c): ranks for a, b, c, ranks in RELAYS}
         ways = [
             [(32 * a + r, 32 * b + r) for a, b in pairs for r in range(32) if r not in away.get((a, b), ())]
@@ -271,8 +288,9 @@
             [(32 * legs[k] + r, 32 * legs[k + 1] + r) for *legs, ranks in RELAYS for r in ranks] for k in range(2)
         ]
         both = ("pulse", "range")
+        passed = lax.ppermute(jnp.where(even, head, tail), both, hops[0])
+        tail, head, *weights = lax.optimization_barrier((tail, head, *weights))
         top, bot = lax.ppermute(tail, both, ways[0]), lax.ppermute(head, both, ways[1])
-        passed = lax.ppermute(jnp.where(even, head, tail), both, hops[0])
         passed = lax.ppermute(passed, both, hops[1])
         ends.append((jnp.where(even, top + passed, top), jnp.where(even, bot, bot + passed)))
     own = own_part(phase_real, phase_imag, weights)

time: 209 us -> 209 us (level)
  starting transfers between devices: 39.9 us -> 54 us
  waiting for transfers between devices: 56.7 us -> 47.4 us
  local copies, waits for them, and re-layouts: 21.5 us -> 14.1 us
  Pallas kernels: 21.5 us -> 25.1 us
    ppermute x1, waiting for transfers between devices: 9.41 us -> 0.07 us  [shards(): lax.ppermute(head, both, ways[1])]
    all_to_all x1, starting transfers between devices: 14.1 us -> 22 us  [shards(): lax.all_to_all(sent, 'range', split_axis=0, concat_axis=0, tiled=True)]
    ppermute x1, starting transfers between devices: 3.43 us -> 9.59 us  [shards(): passed = lax.ppermute(passed, both, hops[1])]
    another operation x4 -> x0, local copies, waits for them, and re-layouts: 5.82 us -> none  [shards(): head = jnp.stack([phase_real[:HALO, columns], phase_imag[:HALO, columns]])]
    all_to_all x1, waiting for transfers between devices: 41.8 us -> 47.3 us  [shards(): lax.all_to_all(sent, 'range', split_axis=0, concat_axis=0, tiled=True)]
    ppermute x1, waiting for transfers between devices: 5.46 us -> 0.01 us  [shards(): passed = lax.ppermute(jnp.where(even, head, tail), both, hops[0])]
    pallas_call x0 -> x2, Pallas kernels: none -> 4.45 us  [block_ends(): pl.pallas_call(ends_kernel, grid=(1,), in_specs=[block(AZ // HALO - 1)] *...]
    another operation x3 -> x0, other arithmetic: 2.74 us -> none  [the longest x2 1.9 us: shards(): jnp.stack([phase_real[AZ - HALO:, columns], phase_imag[AZ - HALO:, column...]
  transfers between devices with their start and end apart: 7 -> 7, of which waited for: 3 -> 2; matrix products, arithmetic and copies ran while one was open for 10% -> 9% of each run, Pallas kernels for 6% -> 7%
where the time goes in v2:
time: 209 us; the launch traced here: 208 us
  blocking collectives  56.8 us (27%)
  starting transfers between devices  54 us (26%)
  waiting for transfers between devices  47.4 us (23%)
  Pallas kernels  25.1 us (12%)
  local copies, waits for them, and re-layouts  14.1 us (7%)
  other arithmetic  9.68 us (5%)
    all_to_all x1, blocking collectives, shards(): lax.all_to_all(sent, 'range', split_axis=0, concat_axis=0, tiled=True)  56.8 us
    all_to_all x1, waiting for transfers between devices, shards(): lax.all_to_all(sent, 'range', split_axis=0, concat_axis=0, tiled=True)  47.3 us
    all_to_all x1, starting transfers between devices, shards(): lax.all_to_all(sent, 'range', split_axis=0, concat_axis=0, tiled=True)  22 us
    ppermute x1, starting transfers between devices, shards(): lax.ppermute(tail, 'pulse', up)  9.66 us
    ppermute x1, starting transfers between devices, shards(): passed = lax.ppermute(passed, both, hops[1])  9.59 us
    ppermute x1, starting transfers between devices, shards(): lax.ppermute(tail, both, ways[0])  8.86 us
    pallas_call x1, Pallas kernels, range_transform(): pl.pallas_call(functools.partial(range_kernel, parts), grid=(4,), in_spec...  8.14 us
    pallas_call x2, Pallas kernels, azimuth(): pl.pallas_call(azimuth_kernel, grid=(width,), in_specs=[pl.BlockSpec((1,...  7.09 us
  transfers between devices with their start and end apart: 7, of which 2 were waited for; matrix products, arithmetic and copies ran while one was open for 9% of the time, Pallas kernels for 7%

profile of v2, /device:TPU:1, one launch (start us, length us, event | category | flops | bytes accessed | tf_op | source)
XLA Modules:
  0.0 208.0 jit_solution(2374199450980951989)
XLA Ops:
  0.6 2.2 %ends.2 = (f32[2,256,256]{2,1,0:T(8,128)}, f32[2,256,256]{2,1,0:T(8,128)}) custom-call(f32[1024,512]{1,0:T(8,128)} %re_ref, f32[1024,512]{1,0:T(8,128)} %im_ref, f32[1024,512]{1,0:T(8,128)} %re_ref, f32[1024,512]{1,0:T(8,128)} %im_ref), custom_call_target="tpu_custom_call" | custom-call | bytes 2097152 | tf_op jit(solution)/shard_map/ends/pallas_call | solution.py:240
  2.8 9.7 %collective-permute-start = (f32[2,256,256]{2,1,0:T(8,128)}, f32[2,256,256]{2,1,0:T(8,128)S(1)}, u32[]{:S(2)}, u32[]{:S(2)}) collective-permute-start(f32[2,256,256]{2,1,0:T(8,128)} %get-tuple-element.24), channel_id=1, source_target_pairs={{0,32},{32,64},{64,96},{96,128},{128,160},{160,192},{192,224},{1,3... | collective-permute-start | bytes 1572872 | tf_op jit(solution)/shard_map/ppermute | solution.py:280
  12.5 1.3 collective-permute-start.1
  13.8 2.3 %ends.3 = (f32[2,256,256]{2,1,0:T(8,128)}, f32[2,256,256]{2,1,0:T(8,128)}) custom-call(f32[1024,512]{1,0:T(8,128)} %re_ref, f32[1024,512]{1,0:T(8,128)} %im_ref, f32[1024,512]{1,0:T(8,128)} %re_ref, f32[1024,512]{1,0:T(8,128)} %im_ref), custom_call_target="tpu_custom_call" | custom-call | bytes 2097152 | tf_op jit(solution)/shard_map/ends/pallas_call | solution.py:240
  16.1 2.0 broadcast_select_fusion
  18.1 1.3 collective-permute-start.3
  19.4 0.1 iota_compare_fusion.2
  19.5 0.1 broadcast_subtract_fusion
  19.5 0.1 and_convert_fusion
  19.6 3.5 %multiply_reduce_fusion = f32[8,5,128,128]{3,2,1,0:T(8,128)S(1)} fusion(f32[8,5,5]{2,1,0:T(8,128)S(1)} %and_convert_fusion, f32[8,5,128,128]{3,2,1,0:T(8,128)} %param.15), kind=kLoop, calls=%fused_computation | loop fusion | flops 5898240 | bytes 5243680 | tf_op jit(solution)/shard_map/reduce_sum | solution.py:259
  23.1 1.5 copy.16
  24.6 3.6 %copy.17 = f32[8,4,32,5,128]{4,3,2,1,0:T(8,128)} copy(f32[8,4,32,5,128]{4,0,1,2,3:T(8,128)S(1)} %bitcast.33) | data formatting | bytes 5242880 | tf_op jit(solution)/shard_map/transpose | solution.py:260
  28.2 4.7 %reshape.47 = f32[8,128,640]{2,1,0:T(8,128)} reshape(f32[8,4,32,5,128]{4,3,2,1,0:T(8,128)} %copy.17) | data formatting | bytes 5242880 | tf_op jit(solution)/shard_map/reshape | solution.py:261
  32.9 2.4 %fusion = (bf16[8,128,640]{2,1,0:T(8,128)(2,1)S(1)}, bf16[8,128,640]{2,1,0:T(8,128)(2,1)S(1)}) fusion(f32[8,128,640]{2,1,0:T(8,128)} %reshape.47), kind=kLoop, calls=%fused_computation.3 | loop fusion | flops 2621440 | bytes 5242880 | tf_op jit(solution)/shard_map/convert_element_type | solution.py:263
  35.3 8.9 %collective-permute-start.2 = (f32[2,256,256]{2,1,0:T(8,128)}, f32[2,256,256]{2,1,0:T(8,128)}, u32[]{:S(2)}, u32[]{:S(2)}) collective-permute-start(f32[2,256,256]{2,1,0:T(8,128)} %get-tuple-element.26), channel_id=1, source_target_pairs={{0,32},{1,33},{2,34},{3,35},{4,36},{5,37},{6,38},{7,39},{8,40},{9,... | collective-permute-start | bytes 1572872 | tf_op jit(solution)/shard_map/ppermute | solution.py:293
  44.2 1.3 collective-permute-start.5
  45.6 0.0 copy-start.4
  45.6 0.0 copy-start.5
  45.6 0.0 copy-start.7
  45.6 5.4 %own.1.own_ref = f32[4,1024,256]{2,1,0:T(8,128)S(1)} custom-call(f32[1024,512]{1,0:T(8,128)S(1)} %copy-done, f32[1024,512]{1,0:T(8,128)S(1)} %copy-done.1, bf16[8,128,640]{2,1,0:T(8,128)(2,1)S(1)} %get-tuple-element.22.wh_ref, bf16[8,128,640]{2,1,0:T(8,128)(2,1)S(1)} %get-tuple-element.23.wl_ref), custom_call_target="tpu_custom_call" | custom-call | flops 1 | bytes 1 | tf_op jit(solution)/shard_map/own/pallas_call | solution.py:99
  51.1 9.6 %collective-permute-start.4 = (f32[2,256,256]{2,1,0:T(8,128)}, f32[2,256,256]{2,1,0:T(8,128)}, u32[]{:S(2)}, u32[]{:S(2)}) collective-permute-start(f32[2,256,256]{2,1,0:T(8,128)} %collective-permute-done.3), channel_id=1, source_target_pairs={{0,32},{1,33},{2,34},{3,35},{4,36},{5,37},{6,38},{7,39},{8,40},{9,... | collective-permute-start | bytes 1572872 | tf_op jit(solution)/shard_map/ppermute | solution.py:294
  60.8 4.0 %azimuth.2 = f32[32,2,2,32,128]{4,3,2,1,0:T(8,128)} custom-call(f32[4,1024,256]{2,1,0:T(8,128)S(1)} %own.1.own_ref, f32[2,256,256]{2,1,0:T(8,128)S(1)} %collective-permute-done.top_ref, f32[2,256,256]{2,1,0:T(8,128)S(1)} %collective-permute-done.1.bot_ref, bf16[2,256,256]{2,1,0:T(8,128)(2,1)S(1)} %pad_maximum_fusion.wh_ref, ...), custom_call_target="tpu_custom_call" | custom-call | flops 3623878656 | bytes 4194304 | tf_op jit(solution)/shard_map/azimuth/pallas_call | solution.py:156
  64.7 2.0 copy-done.2
  66.7 22.0 %all-to-all-start = ((f32[32,2,2,32,128]{4,3,2,1,0:T(8,128)}), f32[32,2,2,32,128]{4,3,2,1,0:T(8,128)}, u32[]{:S(2)}, u32[]{:S(2)}) async-start(f32[32,2,2,32,128]{4,3,2,1,0:T(8,128)} %azimuth.2), calls=%async_computation | async-start | bytes 4194304 | tf_op jit(solution)/shard_map/all_to_all | solution.py:302
  88.7 0.0 copy-start.6
  88.7 0.1 collective-permute-done.5
  88.8 1.5 add_select_fusion
  90.3 2.2 %copy-done.3 = f32[4,1024,256]{2,1,0:T(8,128)S(1)} copy-done((f32[4,1024,256]{2,1,0:T(8,128)S(1)}, f32[4,1024,256]{2,1,0:T(8,128)}, u32[]{:S(2)}) %copy-start.3) | copy-done | bytes 4194328
  92.5 3.1 %azimuth.3 = f32[32,2,2,32,128]{4,3,2,1,0:T(8,128)S(1)} custom-call(f32[4,1024,256]{2,1,0:T(8,128)S(1)} %copy-done.3, f32[2,256,256]{2,1,0:T(8,128)S(1)} %get-tuple-element.41.top_ref, f32[2,256,256]{2,1,0:T(8,128)S(1)} %get-tuple-element.40.bot_ref, bf16[2,256,256]{2,1,0:T(8,128)(2,1)S(1)} %pad_maximum_fusion.wh_ref, ...), custom_call_target="tpu_custom_call" | custom-call | flops 362387865600 | bytes 4194304 | tf_op jit(solution)/shard_map/azimuth/pallas_call | solution.py:156
  95.7 47.3 %all-to-all-done.refs_0_ = f32[32,2,2,32,128]{4,3,2,1,0:T(8,128)} async-done(((f32[32,2,2,32,128]{4,3,2,1,0:T(8,128)}), f32[32,2,2,32,128]{4,3,2,1,0:T(8,128)}, u32[]{:S(2)}, u32[]{:S(2)}) %all-to-all-start) | async-done | bytes 2097184 | tf_op jit(solution)/shard_map/all_to_all | solution.py:302
  143.0 56.8 %all_to_all.10.refs_1_ = f32[32,2,2,32,128]{4,3,2,1,0:T(8,128)S(1)} all-to-all(f32[32,2,2,32,128]{4,3,2,1,0:T(8,128)S(1)} %azimuth.3), channel_id=1, replica_groups=mesh['pulse'=8,'range'=32] {'range'}, dimensions={0} | all-to-all | bytes 4194304 | tf_op jit(solution)/shard_map/all_to_all | solution.py:302
  199.9 8.1 %range.1 = (f32[4,128,8,128]{3,2,1,0:T(8,128)}, f32[4,128,8,128]{3,2,1,0:T(8,128)}) custom-call(f32[32,2,2,32,128]{4,3,2,1,0:T(8,128)} %all-to-all-done.refs_0_, f32[32,2,2,32,128]{4,3,2,1,0:T(8,128)S(1)} %all_to_all.10.refs_1_, bf16[256,256]{1,0:T(8,128)(2,1)S(1)} %copy-done.13, bf16[256,256]{1,0:T(8,128)(2,1)S(1)} %copy-done.12, ...), custom_call_target="tpu_custom_call" | custom-call | flops 1610612736 | bytes 8388608 | tf_op jit(solution)/shard_map/range/pallas_call | solution.py:218
  (43 shorter events, 0.2 us)
Async XLA Ops:
  2.8 57.9 %collective-permute-start = (f32[2,256,256]{2,1,0:T(8,128)}, f32[2,256,256]{2,1,0:T(8,128)S(1)}, u32[]{:S(2)}, u32[]{:S(2)}) collective-permute-start(f32[2,256,256]{2,1,0:T(8,128)} %get-tuple-element.24), channel_id=1, source_target_pairs={{0,32},{32,64},{64,96},{96,128},{128,160},{160,192},{192,224},{1,3... | collective-permute-start | bytes 1572872 | tf_op jit(solution)/shard_map/ppermute | solution.py:280
  12.5 48.2 %collective-permute-start.1 = (f32[2,256,256]{2,1,0:T(8,128)}, f32[2,256,256]{2,1,0:T(8,128)S(1)}, u32[]{:S(2)}, u32[]{:S(2)}) collective-permute-start(f32[2,256,256]{2,1,0:T(8,128)} %get-tuple-element.25), channel_id=1, source_target_pairs={{32,0},{64,32},{96,64},{128,96},{160,128},{192,160},{224,192},{33,... | collective-permute-start | bytes 1572872 | tf_op jit(solution)/shard_map/ppermute | solution.py:280
  13.8 5.6 %copy-start.16 = (s32[8]{0:T(128)S(1)}, s32[8]{0:T(128)}, u32[]{:S(2)}) copy-start(s32[8]{0:T(128)} %param.17) | copy-start | bytes 100
  13.8 5.6 %copy-start.15 = (s32[8,5]{1,0:T(8,128)S(1)}, s32[8,5]{1,0:T(8,128)}, u32[]{:S(2)}) copy-start(s32[8,5]{1,0:T(8,128)} %param.16) | copy-start | bytes 484
  18.1 33.0 %collective-permute-start.3 = (f32[2,256,256]{2,1,0:T(8,128)}, f32[2,256,256]{2,1,0:T(8,128)}, u32[]{:S(2)}, u32[]{:S(2)}) collective-permute-start(f32[2,256,256]{2,1,0:T(8,128)} %broadcast_select_fusion), channel_id=1, source_target_pairs={{64,0},{65,1},{66,2},{67,3},{68,4},{69,5},{70,6},{71,7},{72,8},{73... | collective-permute-start | bytes 1572872 | tf_op jit(solution)/shard_map/ppermute | solution.py:291
  32.9 11.2 %copy-start.14 = (f32[2,256,256]{2,1,0:T(8,128)S(1)}, f32[2,256,256]{2,1,0:T(8,128)}, u32[]{:S(2)}) copy-start(f32[2,256,256]{2,1,0:T(8,128)} %get-tuple-element.27) | copy-start | bytes 1572868
  32.9 12.6 %copy-start = (f32[1024,512]{1,0:T(8,128)S(1)}, f32[1024,512]{1,0:T(8,128)}, u32[]{:S(2)}) copy-start(f32[1024,512]{1,0:T(8,128)} %re_ref) | copy-start | bytes 6291460
  32.9 12.7 %copy-start.1 = (f32[1024,512]{1,0:T(8,128)S(1)}, f32[1024,512]{1,0:T(8,128)}, u32[]{:S(2)}) copy-start(f32[1024,512]{1,0:T(8,128)} %im_ref) | copy-start | bytes 6291460
  35.3 53.4 %collective-permute-start.2 = (f32[2,256,256]{2,1,0:T(8,128)}, f32[2,256,256]{2,1,0:T(8,128)}, u32[]{:S(2)}, u32[]{:S(2)}) collective-permute-start(f32[2,256,256]{2,1,0:T(8,128)} %get-tuple-element.26), channel_id=1, source_target_pairs={{0,32},{1,33},{2,34},{3,35},{4,36},{5,37},{6,38},{7,39},{8,40},{9,... | collective-permute-start | bytes 1572872 | tf_op jit(solution)/shard_map/ppermute | solution.py:293
  44.2 44.6 %collective-permute-start.5 = (f32[2,256,256]{2,1,0:T(8,128)S(1)}, f32[2,256,256]{2,1,0:T(8,128)}, u32[]{:S(2)}, u32[]{:S(2)}) collective-permute-start(f32[2,256,256]{2,1,0:T(8,128)S(1)} %copy-done.14), channel_id=1, source_target_pairs={{32,0},{33,1},{34,2},{35,3},{36,4},{37,5},{38,6},{39,7},{40,8},{41... | collective-permute-start | bytes 1572872 | tf_op jit(solution)/shard_map/ppermute | solution.py:293
  45.6 15.2 %copy-start.4 = (f32[3,2,256,128]{3,2,1,0:T(8,128)S(1)}, f32[3,2,256,128]{3,2,1,0:T(8,128)}, u32[]{:S(2)}) copy-start(f32[3,2,256,128]{3,2,1,0:T(8,128)} %constant.46.clone.tw_ref) | copy-start | bytes 2359300
  45.6 15.2 %copy-start.5 = (bf16[512,256]{1,0:T(8,128)(2,1)S(1)}, bf16[512,256]{1,0:T(8,128)(2,1)}, u32[]{:S(2)}) copy-start(bf16[512,256]{1,0:T(8,128)(2,1)} %constant.45.clone.dl_ref) | copy-start | bytes 786436
  45.6 15.2 %copy-start.7 = (bf16[512,256]{1,0:T(8,128)(2,1)S(1)}, bf16[512,256]{1,0:T(8,128)(2,1)}, u32[]{:S(2)}) copy-start(bf16[512,256]{1,0:T(8,128)(2,1)} %constant.44.clone.dh_ref) | copy-start | bytes 786436
  51.1 37.7 %collective-permute-start.4 = (f32[2,256,256]{2,1,0:T(8,128)}, f32[2,256,256]{2,1,0:T(8,128)}, u32[]{:S(2)}, u32[]{:S(2)}) collective-permute-start(f32[2,256,256]{2,1,0:T(8,128)} %collective-permute-done.3), channel_id=1, source_target_pairs={{0,32},{1,33},{2,34},{3,35},{4,36},{5,37},{6,38},{7,39},{8,40},{9,... | collective-permute-start | bytes 1572872 | tf_op jit(solution)/shard_map/ppermute | solution.py:294
  64.7 2.0 copy-start.2
  66.7 76.4 %all-to-all-start = ((f32[32,2,2,32,128]{4,3,2,1,0:T(8,128)}), f32[32,2,2,32,128]{4,3,2,1,0:T(8,128)}, u32[]{:S(2)}, u32[]{:S(2)}) async-start(f32[32,2,2,32,128]{4,3,2,1,0:T(8,128)} %azimuth.2), calls=%async_computation | async-start | bytes 4194304 | tf_op jit(solution)/shard_map/all_to_all | solution.py:302
  88.7 1.6 copy-start.6
  88.7 1.6 copy-start.8
  90.3 2.2 %copy-start.3 = (f32[4,1024,256]{2,1,0:T(8,128)S(1)}, f32[4,1024,256]{2,1,0:T(8,128)}, u32[]{:S(2)}) copy-start(f32[4,1024,256]{2,1,0:T(8,128)} %copy-done.2) | copy-start | bytes 12582916
  95.7 104.2 %copy-start.9 = (bf16[256,256]{1,0:T(8,128)(2,1)S(1)}, bf16[256,256]{1,0:T(8,128)(2,1)}, u32[]{:S(2)}) copy-start(bf16[256,256]{1,0:T(8,128)(2,1)} %constant.51.clone.refs_6_) | copy-start | bytes 393220
  95.7 104.2 %copy-start.10 = (bf16[256,256]{1,0:T(8,128)(2,1)S(1)}, bf16[256,256]{1,0:T(8,128)(2,1)}, u32[]{:S(2)}) copy-start(bf16[256,256]{1,0:T(8,128)(2,1)} %constant.50.clone.refs_5_) | copy-start | bytes 393220
  95.7 104.2 %copy-start.11 = (f32[2,128,128]{2,1,0:T(8,128)S(1)}, f32[2,128,128]{2,1,0:T(8,128)}, u32[]{:S(2)}) copy-start(f32[2,128,128]{2,1,0:T(8,128)} %constant.49.clone.refs_4_) | copy-start | bytes 393220
  95.7 104.1 %copy-start.12 = (bf16[256,256]{1,0:T(8,128)(2,1)S(1)}, bf16[256,256]{1,0:T(8,128)(2,1)}, u32[]{:S(2)}) copy-start(bf16[256,256]{1,0:T(8,128)(2,1)} %constant.48.clone.refs_3_) | copy-start | bytes 393220
  95.7 104.1 %copy-start.13 = (bf16[256,256]{1,0:T(8,128)(2,1)S(1)}, bf16[256,256]{1,0:T(8,128)(2,1)}, u32[]{:S(2)}) copy-start(bf16[256,256]{1,0:T(8,128)(2,1)} %constant.47.clone.refs_2_) | copy-start | bytes 393220

commit v3 on v2

--- a/solution.py
+++ b/solution.py
@@ -289,12 +289,12 @@
         ]
         both = ("pulse", "range")
         passed = lax.ppermute(jnp.where(even, head, tail), both, hops[0])
-        tail, head, *weights = lax.optimization_barrier((tail, head, *weights))
+        own = own_part(phase_real, phase_imag, weights)
+        edges = [edge_weights(half) for half in weights]
+        tail, head, own, *edges = lax.optimization_barrier((tail, head, own, *edges))
         top, bot = lax.ppermute(tail, both, ways[0]), lax.ppermute(head, both, ways[1])
         passed = lax.ppermute(passed, both, hops[1])
         ends.append((jnp.where(even, top + passed, top), jnp.where(even, bot, bot + passed)))
-    own = own_part(phase_real, phase_imag, weights)
-    edges = [edge_weights(half) for half in weights]
     cells = []
     first = 0
     for width, (top, bot) in zip(PARTS, ends):

time: 209 us -> 209 us (level)
  waiting for transfers between devices: 47.4 us -> 57.9 us
  starting transfers between devices: 54 us -> 44.3 us
    ppermute x1, waiting for transfers between devices: 0.07 us -> 16.4 us  [shards(): lax.ppermute(head, both, ways[1])]
    all_to_all x1, starting transfers between devices: 22 us -> 12.3 us  [shards(): lax.all_to_all(sent, 'range', split_axis=0, concat_axis=0, tiled=True)]
    all_to_all x1, waiting for transfers between devices: 47.3 us -> 41.2 us  [shards(): lax.all_to_all(sent, 'range', split_axis=0, concat_axis=0, tiled=True)]
  transfers between devices with their start and end apart: 7 -> 7, of which waited for: 2 -> 3; matrix products, arithmetic and copies ran while one was open for 9% -> 9% of each run, Pallas kernels for 7% -> 7%
where the time goes in v3:
time: 209 us; the launch traced here: 208 us
  waiting for transfers between devices  57.9 us (28%)
  blocking collectives  55.8 us (27%)
  starting transfers between devices  44.3 us (21%)
  Pallas kernels  25 us (12%)
  local copies, waits for them, and re-layouts  14.6 us (7%)
  other arithmetic  9.64 us (5%)
    all_to_all x1, blocking collectives, shards(): lax.all_to_all(sent, 'range', split_axis=0, concat_axis=0, tiled=True)  55.8 us
    all_to_all x1, waiting for transfers between devices, shards(): lax.all_to_all(sent, 'range', split_axis=0, concat_axis=0, tiled=True)  41.2 us
    ppermute x1, waiting for transfers between devices, shards(): lax.ppermute(head, both, ways[1])  16.4 us
    all_to_all x1, starting transfers between devices, shards(): lax.all_to_all(sent, 'range', split_axis=0, concat_axis=0, tiled=True)  12.3 us
    ppermute x1, starting transfers between devices, shards(): lax.ppermute(tail, 'pulse', up)  9.66 us
    ppermute x1, starting transfers between devices, shards(): passed = lax.ppermute(passed, both, hops[1])  9.6 us
    ppermute x1, starting transfers between devices, shards(): lax.ppermute(tail, both, ways[0])  8.88 us
    pallas_call x1, Pallas kernels, range_transform(): pl.pallas_call(functools.partial(range_kernel, parts), grid=(4,), in_spec...  8.14 us
  transfers between devices with their start and end apart: 7, of which 3 were waited for; matrix products, arithmetic and copies ran while one was open for 9% of the time, Pallas kernels for 7%

profile of v3, /device:TPU:1, one launch (start us, length us, event | category | flops | bytes accessed | tf_op | source)
XLA Modules:
  0.0 208.2 jit_solution(16391110753023406836)
XLA Ops:
  0.6 2.2 %ends.2 = (f32[2,256,256]{2,1,0:T(8,128)}, f32[2,256,256]{2,1,0:T(8,128)}) custom-call(f32[1024,512]{1,0:T(8,128)} %re_ref, f32[1024,512]{1,0:T(8,128)} %im_ref, f32[1024,512]{1,0:T(8,128)} %re_ref, f32[1024,512]{1,0:T(8,128)} %im_ref), custom_call_target="tpu_custom_call" | custom-call | bytes 2097152 | tf_op jit(solution)/shard_map/ends/pallas_call | solution.py:240
  2.8 9.7 %collective-permute-start = (f32[2,256,256]{2,1,0:T(8,128)}, f32[2,256,256]{2,1,0:T(8,128)S(1)}, u32[]{:S(2)}, u32[]{:S(2)}) collective-permute-start(f32[2,256,256]{2,1,0:T(8,128)} %get-tuple-element.24), channel_id=1, source_target_pairs={{0,32},{32,64},{64,96},{96,128},{128,160},{160,192},{192,224},{1,3... | collective-permute-start | bytes 1572872 | tf_op jit(solution)/shard_map/ppermute | solution.py:280
  12.5 1.3 collective-permute-start.1
  13.8 2.3 %ends.3 = (f32[2,256,256]{2,1,0:T(8,128)}, f32[2,256,256]{2,1,0:T(8,128)}) custom-call(f32[1024,512]{1,0:T(8,128)} %re_ref, f32[1024,512]{1,0:T(8,128)} %im_ref, f32[1024,512]{1,0:T(8,128)} %re_ref, f32[1024,512]{1,0:T(8,128)} %im_ref), custom_call_target="tpu_custom_call" | custom-call | bytes 2097152 | tf_op jit(solution)/shard_map/ends/pallas_call | solution.py:240
  16.1 2.0 broadcast_select_fusion
  18.1 1.3 collective-permute-start.3
  19.4 0.1 iota_compare_fusion.2
  19.5 0.1 broadcast_subtract_fusion
  19.5 0.1 and_convert_fusion
  19.6 3.5 %multiply_reduce_fusion = f32[8,5,128,128]{3,2,1,0:T(8,128)S(1)} fusion(f32[8,5,5]{2,1,0:T(8,128)S(1)} %and_convert_fusion, f32[8,5,128,128]{3,2,1,0:T(8,128)} %param.15), kind=kLoop, calls=%fused_computation | loop fusion | flops 5898240 | bytes 5243680 | tf_op jit(solution)/shard_map/reduce_sum | solution.py:259
  23.1 1.5 copy.16
  24.6 3.6 %copy.17 = f32[8,4,32,5,128]{4,3,2,1,0:T(8,128)} copy(f32[8,4,32,5,128]{4,0,1,2,3:T(8,128)S(1)} %bitcast.33) | data formatting | bytes 5242880 | tf_op jit(solution)/shard_map/transpose | solution.py:260
  28.2 4.7 %reshape.47 = f32[8,128,640]{2,1,0:T(8,128)} reshape(f32[8,4,32,5,128]{4,3,2,1,0:T(8,128)} %copy.17) | data formatting | bytes 5242880 | tf_op jit(solution)/shard_map/reshape | solution.py:261
  32.9 2.4 %fusion = (bf16[8,128,640]{2,1,0:T(8,128)(2,1)S(1)}, bf16[8,128,640]{2,1,0:T(8,128)(2,1)S(1)}) fusion(f32[8,128,640]{2,1,0:T(8,128)} %reshape.47), kind=kLoop, calls=%fused_computation.3 | loop fusion | flops 2621440 | bytes 5242880 | tf_op jit(solution)/shard_map/convert_element_type | solution.py:263
  35.4 0.5 copy-done.1
  35.9 5.4 %own.1.own_ref = f32[4,1024,256]{2,1,0:T(8,128)S(1)} custom-call(f32[1024,512]{1,0:T(8,128)S(1)} %copy-done, f32[1024,512]{1,0:T(8,128)S(1)} %copy-done.1, bf16[8,128,640]{2,1,0:T(8,128)(2,1)S(1)} %get-tuple-element.33.wh_ref, bf16[8,128,640]{2,1,0:T(8,128)(2,1)S(1)} %get-tuple-element.32.wl_ref), custom_call_target="tpu_custom_call" | custom-call | flops 1 | bytes 1 | tf_op jit(solution)/shard_map/own/pallas_call | solution.py:99
  41.4 8.9 %collective-permute-start.2 = (f32[2,256,256]{2,1,0:T(8,128)}, f32[2,256,256]{2,1,0:T(8,128)}, u32[]{:S(2)}, u32[]{:S(2)}) collective-permute-start(f32[2,256,256]{2,1,0:T(8,128)} %get-tuple-element.28), channel_id=1, source_target_pairs={{0,32},{1,33},{2,34},{3,35},{4,36},{5,37},{6,38},{7,39},{8,40},{9,... | collective-permute-start | bytes 1572872 | tf_op jit(solution)/shard_map/ppermute | solution.py:295
  50.3 1.3 collective-permute-start.5
  51.6 9.6 %collective-permute-start.4 = (f32[2,256,256]{2,1,0:T(8,128)}, f32[2,256,256]{2,1,0:T(8,128)}, u32[]{:S(2)}, u32[]{:S(2)}) collective-permute-start(f32[2,256,256]{2,1,0:T(8,128)} %collective-permute-done.3), channel_id=1, source_target_pairs={{0,32},{1,33},{2,34},{3,35},{4,36},{5,37},{6,38},{7,39},{8,40},{9,... | collective-permute-start | bytes 1572872 | tf_op jit(solution)/shard_map/ppermute | solution.py:296
  61.2 4.0 %azimuth.2 = f32[32,2,2,32,128]{4,3,2,1,0:T(8,128)} custom-call(f32[4,1024,256]{2,1,0:T(8,128)S(1)} %own.1.own_ref, f32[2,256,256]{2,1,0:T(8,128)S(1)} %collective-permute-done.top_ref, f32[2,256,256]{2,1,0:T(8,128)S(1)} %collective-permute-done.1.bot_ref, bf16[2,256,256]{2,1,0:T(8,128)(2,1)S(1)} %pad_maximum_fusion.wh_ref, ...), custom_call_target="tpu_custom_call" | custom-call | flops 3623878656 | bytes 4194304 | tf_op jit(solution)/shard_map/azimuth/pallas_call | solution.py:156
  65.2 2.0 copy-done.2
  67.2 12.3 %all-to-all-start = ((f32[32,2,2,32,128]{4,3,2,1,0:T(8,128)}), f32[32,2,2,32,128]{4,3,2,1,0:T(8,128)}, u32[]{:S(2)}, u32[]{:S(2)}) async-start(f32[32,2,2,32,128]{4,3,2,1,0:T(8,128)} %azimuth.2), calls=%async_computation | async-start | bytes 4194304 | tf_op jit(solution)/shard_map/all_to_all | solution.py:302
  79.4 0.0 copy-start.6
  79.4 0.0 copy-start.8
  79.5 16.4 %collective-permute-done.5 = f32[2,256,256]{2,1,0:T(8,128)} collective-permute-done((f32[2,256,256]{2,1,0:T(8,128)S(1)}, f32[2,256,256]{2,1,0:T(8,128)}, u32[]{:S(2)}, u32[]{:S(2)}) %collective-permute-start.5) | collective-permute-done | bytes 524320 | tf_op jit(solution)/shard_map/ppermute | solution.py:295
  95.9 0.3 collective-permute-done.4
  96.1 1.5 add_select_fusion
  97.6 2.2 %copy-done.3 = f32[4,1024,256]{2,1,0:T(8,128)S(1)} copy-done((f32[4,1024,256]{2,1,0:T(8,128)S(1)}, f32[4,1024,256]{2,1,0:T(8,128)}, u32[]{:S(2)}) %copy-start.3) | copy-done | bytes 4194328
  99.8 3.1 %azimuth.3 = f32[32,2,2,32,128]{4,3,2,1,0:T(8,128)S(1)} custom-call(f32[4,1024,256]{2,1,0:T(8,128)S(1)} %copy-done.3, f32[2,256,256]{2,1,0:T(8,128)S(1)} %get-tuple-element.43.top_ref, f32[2,256,256]{2,1,0:T(8,128)S(1)} %get-tuple-element.42.bot_ref, bf16[2,256,256]{2,1,0:T(8,128)(2,1)S(1)} %pad_maximum_fusion.wh_ref, ...), custom_call_target="tpu_custom_call" | custom-call | flops 362387865600 | bytes 4194304 | tf_op jit(solution)/shard_map/azimuth/pallas_call | solution.py:156
  103.0 41.2 %all-to-all-done.refs_0_ = f32[32,2,2,32,128]{4,3,2,1,0:T(8,128)} async-done(((f32[32,2,2,32,128]{4,3,2,1,0:T(8,128)}), f32[32,2,2,32,128]{4,3,2,1,0:T(8,128)}, u32[]{:S(2)}, u32[]{:S(2)}) %all-to-all-start) | async-done | bytes 2097184 | tf_op jit(solution)/shard_map/all_to_all | solution.py:302
  144.2 55.8 %all_to_all.10.refs_1_ = f32[32,2,2,32,128]{4,3,2,1,0:T(8,128)S(1)} all-to-all(f32[32,2,2,32,128]{4,3,2,1,0:T(8,128)S(1)} %azimuth.3), channel_id=1, replica_groups=mesh['pulse'=8,'range'=32] {'range'}, dimensions={0} | all-to-all | bytes 4194304 | tf_op jit(solution)/shard_map/all_to_all | solution.py:302
  200.0 8.1 %range.1 = (f32[4,128,8,128]{3,2,1,0:T(8,128)}, f32[4,128,8,128]{3,2,1,0:T(8,128)}) custom-call(f32[32,2,2,32,128]{4,3,2,1,0:T(8,128)} %all-to-all-done.refs_0_, f32[32,2,2,32,128]{4,3,2,1,0:T(8,128)S(1)} %all_to_all.10.refs_1_, bf16[256,256]{1,0:T(8,128)(2,1)S(1)} %copy-done.13, bf16[256,256]{1,0:T(8,128)(2,1)S(1)} %copy-done.12, ...), custom_call_target="tpu_custom_call" | custom-call | flops 1610612736 | bytes 8388608 | tf_op jit(solution)/shard_map/range/pallas_call | solution.py:218
  (43 shorter events, 0.2 us)
Async XLA Ops:
  2.8 58.4 %collective-permute-start = (f32[2,256,256]{2,1,0:T(8,128)}, f32[2,256,256]{2,1,0:T(8,128)S(1)}, u32[]{:S(2)}, u32[]{:S(2)}) collective-permute-start(f32[2,256,256]{2,1,0:T(8,128)} %get-tuple-element.24), channel_id=1, source_target_pairs={{0,32},{32,64},{64,96},{96,128},{128,160},{160,192},{192,224},{1,3... | collective-permute-start | bytes 1572872 | tf_op jit(solution)/shard_map/ppermute | solution.py:280
  12.5 48.7 %collective-permute-start.1 = (f32[2,256,256]{2,1,0:T(8,128)}, f32[2,256,256]{2,1,0:T(8,128)S(1)}, u32[]{:S(2)}, u32[]{:S(2)}) collective-permute-start(f32[2,256,256]{2,1,0:T(8,128)} %get-tuple-element.25), channel_id=1, source_target_pairs={{32,0},{64,32},{96,64},{128,96},{160,128},{192,160},{224,192},{33,... | collective-permute-start | bytes 1572872 | tf_op jit(solution)/shard_map/ppermute | solution.py:280
  13.8 5.6 %copy-start.16 = (s32[8]{0:T(128)S(1)}, s32[8]{0:T(128)}, u32[]{:S(2)}) copy-start(s32[8]{0:T(128)} %param.17) | copy-start | bytes 100
  13.8 5.6 %copy-start.15 = (s32[8,5]{1,0:T(8,128)S(1)}, s32[8,5]{1,0:T(8,128)}, u32[]{:S(2)}) copy-start(s32[8,5]{1,0:T(8,128)} %param.16) | copy-start | bytes 484
  18.1 33.5 %collective-permute-start.3 = (f32[2,256,256]{2,1,0:T(8,128)}, f32[2,256,256]{2,1,0:T(8,128)}, u32[]{:S(2)}, u32[]{:S(2)}) collective-permute-start(f32[2,256,256]{2,1,0:T(8,128)} %broadcast_select_fusion), channel_id=1, source_target_pairs={{64,0},{65,1},{66,2},{67,3},{68,4},{69,5},{70,6},{71,7},{72,8},{73... | collective-permute-start | bytes 1572872 | tf_op jit(solution)/shard_map/ppermute | solution.py:291
  32.9 2.5 %copy-start = (f32[1024,512]{1,0:T(8,128)S(1)}, f32[1024,512]{1,0:T(8,128)}, u32[]{:S(2)}) copy-start(f32[1024,512]{1,0:T(8,128)} %re_ref) | copy-start | bytes 6291460
  32.9 3.0 %copy-start.1 = (f32[1024,512]{1,0:T(8,128)S(1)}, f32[1024,512]{1,0:T(8,128)}, u32[]{:S(2)}) copy-start(f32[1024,512]{1,0:T(8,128)} %im_ref) | copy-start | bytes 6291460
  35.9 14.4 %copy-start.14 = (f32[2,256,256]{2,1,0:T(8,128)S(1)}, f32[2,256,256]{2,1,0:T(8,128)}, u32[]{:S(2)}) copy-start(f32[2,256,256]{2,1,0:T(8,128)} %get-tuple-element.29) | copy-start | bytes 1572868
  35.9 25.3 %copy-start.4 = (f32[3,2,256,128]{3,2,1,0:T(8,128)S(1)}, f32[3,2,256,128]{3,2,1,0:T(8,128)}, u32[]{:S(2)}) copy-start(f32[3,2,256,128]{3,2,1,0:T(8,128)} %constant.46.clone.tw_ref) | copy-start | bytes 2359300
  35.9 25.3 %copy-start.5 = (bf16[512,256]{1,0:T(8,128)(2,1)S(1)}, bf16[512,256]{1,0:T(8,128)(2,1)}, u32[]{:S(2)}) copy-start(bf16[512,256]{1,0:T(8,128)(2,1)} %constant.45.clone.dl_ref) | copy-start | bytes 786436
  35.9 25.3 %copy-start.7 = (bf16[512,256]{1,0:T(8,128)(2,1)S(1)}, bf16[512,256]{1,0:T(8,128)(2,1)}, u32[]{:S(2)}) copy-start(bf16[512,256]{1,0:T(8,128)(2,1)} %constant.44.clone.dh_ref) | copy-start | bytes 786436
  41.4 38.0 %collective-permute-start.2 = (f32[2,256,256]{2,1,0:T(8,128)}, f32[2,256,256]{2,1,0:T(8,128)}, u32[]{:S(2)}, u32[]{:S(2)}) collective-permute-start(f32[2,256,256]{2,1,0:T(8,128)} %get-tuple-element.28), channel_id=1, source_target_pairs={{0,32},{1,33},{2,34},{3,35},{4,36},{5,37},{6,38},{7,39},{8,40},{9,... | collective-permute-start | bytes 1572872 | tf_op jit(solution)/shard_map/ppermute | solution.py:295
  50.3 45.6 %collective-permute-start.5 = (f32[2,256,256]{2,1,0:T(8,128)S(1)}, f32[2,256,256]{2,1,0:T(8,128)}, u32[]{:S(2)}, u32[]{:S(2)}) collective-permute-start(f32[2,256,256]{2,1,0:T(8,128)S(1)} %copy-done.14), channel_id=1, source_target_pairs={{32,0},{33,1},{34,2},{35,3},{36,4},{37,5},{38,6},{39,7},{40,8},{41... | collective-permute-start | bytes 1572872 | tf_op jit(solution)/shard_map/ppermute | solution.py:295
  51.6 44.5 %collective-permute-start.4 = (f32[2,256,256]{2,1,0:T(8,128)}, f32[2,256,256]{2,1,0:T(8,128)}, u32[]{:S(2)}, u32[]{:S(2)}) collective-permute-start(f32[2,256,256]{2,1,0:T(8,128)} %collective-permute-done.3), channel_id=1, source_target_pairs={{0,32},{1,33},{2,34},{3,35},{4,36},{5,37},{6,38},{7,39},{8,40},{9,... | collective-permute-start | bytes 1572872 | tf_op jit(solution)/shard_map/ppermute | solution.py:296
  65.2 2.0 copy-start.2
  67.2 77.1 %all-to-all-start = ((f32[32,2,2,32,128]{4,3,2,1,0:T(8,128)}), f32[32,2,2,32,128]{4,3,2,1,0:T(8,128)}, u32[]{:S(2)}, u32[]{:S(2)}) async-start(f32[32,2,2,32,128]{4,3,2,1,0:T(8,128)} %azimuth.2), calls=%async_computation | async-start | bytes 4194304 | tf_op jit(solution)/shard_map/all_to_all | solution.py:302
  79.4 18.1 %copy-start.6 = (bf16[512,256]{1,0:T(8,128)(2,1)S(1)}, bf16[512,256]{1,0:T(8,128)(2,1)}, u32[]{:S(2)}) copy-start(bf16[512,256]{1,0:T(8,128)(2,1)} %constant.45.clone.dl_ref) | copy-start | bytes 786436
  79.4 18.1 %copy-start.8 = (bf16[512,256]{1,0:T(8,128)(2,1)S(1)}, bf16[512,256]{1,0:T(8,128)(2,1)}, u32[]{:S(2)}) copy-start(bf16[512,256]{1,0:T(8,128)(2,1)} %constant.44.clone.dh_ref) | copy-start | bytes 786436
  97.6 2.2 %copy-start.3 = (f32[4,1024,256]{2,1,0:T(8,128)S(1)}, f32[4,1024,256]{2,1,0:T(8,128)}, u32[]{:S(2)}) copy-start(f32[4,1024,256]{2,1,0:T(8,128)} %copy-done.2) | copy-start | bytes 12582916
  102.9 97.1 %copy-start.9 = (bf16[256,256]{1,0:T(8,128)(2,1)S(1)}, bf16[256,256]{1,0:T(8,128)(2,1)}, u32[]{:S(2)}) copy-start(bf16[256,256]{1,0:T(8,128)(2,1)} %constant.51.clone.refs_6_) | copy-start | bytes 393220
  102.9 97.1 %copy-start.10 = (bf16[256,256]{1,0:T(8,128)(2,1)S(1)}, bf16[256,256]{1,0:T(8,128)(2,1)}, u32[]{:S(2)}) copy-start(bf16[256,256]{1,0:T(8,128)(2,1)} %constant.50.clone.refs_5_) | copy-start | bytes 393220
  102.9 97.1 %copy-start.11 = (f32[2,128,128]{2,1,0:T(8,128)S(1)}, f32[2,128,128]{2,1,0:T(8,128)}, u32[]{:S(2)}) copy-start(f32[2,128,128]{2,1,0:T(8,128)} %constant.49.clone.refs_4_) | copy-start | bytes 393220
  103.0 97.1 %copy-start.12 = (bf16[256,256]{1,0:T(8,128)(2,1)S(1)}, bf16[256,256]{1,0:T(8,128)(2,1)}, u32[]{:S(2)}) copy-start(bf16[256,256]{1,0:T(8,128)(2,1)} %constant.48.clone.refs_3_) | copy-start | bytes 393220
  103.0 97.1 %copy-start.13 = (bf16[256,256]{1,0:T(8,128)(2,1)S(1)}, bf16[256,256]{1,0:T(8,128)(2,1)}, u32[]{:S(2)}) copy-start(bf16[256,256]{1,0:T(8,128)(2,1)} %constant.47.clone.refs_2_) | copy-start | bytes 393220
